TPU v7x, 32 devices: a whole 2x2x4 slice. The times are simulated.
32 devices in a mesh: row: 8 (over z, x), col: 4 (over y, core).
Axes of the slice: x: 2, y: 2, z: 4, core: 2. Of those that a mesh axis runs over, the one named last changes fastest.
Arguments:
- features: bfloat16 [192, 52, 2048], P('row', 'col'), may hold values from -6 to 6
- crop_rows: int32 [5], replicated, may hold values from 1 to 49, 192 in all
- crop_cols: int32 [5], replicated, may hold values from 25 to 49
- w_point: bfloat16 [2048, 256], P('row'), may hold values from -0.125 to 0.125
- w_atrous: bfloat16 [2048, 27, 256], P('row'), may hold values from -0.046875 to 0.046875
- w_pool: bfloat16 [2048, 256], P('row'), may hold values from -0.125 to 0.125
- w_proj: bfloat16 [1280, 256], P('row'), may hold values from -0.15625 to 0.15625
- gains: float32 [6, 256], replicated, may hold values from 0.5 to 1.5
- biases: float32 [6, 256], replicated, may hold values from -3 to 3
- cotangent: bfloat16 [192, 52, 256], P('row', 'col'), may hold values from -6 to 6
Outputs:
- result: bfloat16 [192, 52, 256], P('row', 'col')
- d_features: bfloat16 [192, 52, 2048], P('row', 'col')
- d_point: float32 [2048, 256], P('row')
- d_atrous: float32 [2048, 27, 256], P('row')
- d_pool: float32 [2048, 256], P('row')
- d_proj: float32 [1280, 256], P('row')
- d_gains: float32 [6, 256], replicated
- d_biases: float32 [6, 256], replicated
Inputs may be any that keep to these rules, and one draw needn't show every extreme that they name: `crop_rows`: crop heights sum to 192; the tallest crop has 49 rows.
All inputs are finite; a program needn't handle non-finite values.
Results may differ from a plain program's by a relative error of at most 0.02.
Values may be sent and summed in bfloat16 or wider, within the bound.
A program may use at most 384 MiB of HBM per device.

v0:
```python
import functools

import jax
import jax.numpy as jnp
import numpy as np
from jax import lax
from jax.experimental import pallas as pl
from jax.experimental.pallas import tpu as pltpu
from jax.sharding import PartitionSpec as P

EPSILON = 1e-05
MARGIN = 18
DILATIONS = (6, 12, 18)
MEMBERS = 8
TAPS = 30
POINT, POOL, GROUPS = 27, 28, 10
MESH = pl.DeviceIdType.MESH
F32 = jnp.float32
BF16 = jnp.bfloat16

def up_to(value, multiple):
    return -(-value // multiple) * multiple


class Plan:
    def __init__(self, rows_axis, cols_axis, h, bc, channels, width, crops):
        self.R, self.C = rows_axis, cols_axis
        self.h, self.bc, self.channels, self.width = h, bc, channels, width
        self.G = MEMBERS // self.C
        self.slabs = self.R // self.G
        self.H = self.G * h
        self.cols = bc * self.C
        self.S = up_to(self.cols, 8)
        self.rpb = self.H // MEMBERS
        self.px = self.rpb * self.S
        self.own = MEMBERS * self.px
        self.hb = MARGIN // self.rpb
        self.nb = MEMBERS + 2 * self.hb
        self.ext = self.nb * self.px
        self.bp = up_to(bc, 16)
        self.cs = channels // MEMBERS
        self.crops = crops
        self.ncp = up_to(crops, 16)
        self.exchange = self.slabs == self.C and self.R == MEMBERS
        self.steps = tuple(d // self.rpb for d in DILATIONS)
        self.proj = 5 * width // self.R
        self.piece = up_to(self.proj // self.C, 16)


def home_of(pn, col):
    if pn.C != 4:
        return col
    y, c = col // 2, lax.rem(col, 2)
    return (1 - y) * 3 * c + y * (1 + c)


def slice_of(pn, k):
    return pn.G * home_of(pn, lax.rem(k, pn.C)) + k // pn.C


def remote(src, dst, send, recv, device):
    return pltpu.make_async_remote_copy(
        src_ref=src, dst_ref=dst, send_sem=send, recv_sem=recv, device_id=device, device_id_type=MESH
    )


def greet_all(pn, row, col):
    total = pn.R * pn.C
    barrier = pltpu.get_barrier_semaphore()
    me = row * pn.C + col

    def hello(k, carry):
        other = lax.rem(me + k, total)
        pl.semaphore_signal(
            barrier, inc=1, device_id=(other // pn.C, lax.rem(other, pn.C)), device_id_type=MESH
        )
        return carry

    lax.fori_loop(1, total, hello, 0)
    pl.semaphore_wait(barrier, total - 1)


def dot(a, b):
    return jnp.dot(a, b, preferred_element_type=F32)


def dot_nt(a, b):
    return lax.dot_general(a, b, (((1,), (1,)), ((), ())), preferred_element_type=F32)


def dot_tn(a, b):
    return lax.dot_general(a, b, (((0,), (0,)), ((), ())), preferred_element_type=F32)


def split_dot(dot_fn, a, b):
    high = a.astype(BF16)
    low = (a - high.astype(F32)).astype(BF16)
    return dot_fn(high, b) + dot_fn(low, b)


def conv_kernel(pn, feats, w_in, cot, proj, masks, sel, hot_t, inv_counts,
                p_out, x_out, w_out, m_out, p4_out, cot_out, proj_out,
                ring, xs, wbuf, acc, pbuf, cbuf, sbuf, rbuf, cx,
                f_s, f_r, h_s, h_r, c_s, c_r, j_s, j_r, t_s, t_r, w_s, w_r, w_l, e_s,
                r1_s, r1_r, r2_s, r2_r, o_s):
    row, col = lax.axis_index("row"), lax.axis_index("col")
    slab, x = row // pn.G, lax.rem(row, pn.G)
    me = x * pn.C + col
    core, quad = lax.rem(col, 2), me // 2
    h, H, bp, px, n = pn.h, pn.H, pn.bp, pn.px, pn.slabs
    many = 4

    def member(s, k):
        return (s * pn.G + k // pn.C, lax.rem(k, pn.C))

    greet_all(pn, row, col)

    own_cols = pl.ds(pl.multiple_of(col * bp, bp), bp)
    own_rows = pl.ds(MARGIN + h * x, h)
    sent = []
    for kk in range(1, MEMBERS):
        other = lax.rem(me + kk, MEMBERS)
        c = remote(feats.at[slice_of(pn, other)], ring.at[own_rows, own_cols], f_s.at[kk], f_r.at[kk], member(slab, other))
        c.start()
        sent.append(c)
    keep = pltpu.make_async_copy(feats.at[slice_of(pn, me)], ring.at[own_rows, own_cols], f_r.at[0])
    keep.start()

    home = home_of(pn, col)
    source, rising, falling = slab == home, (slab > home) & (slab < n - 1), (slab < home) & (slab > 0)
    help_up, help_down = (slab == n - 2) & (col == 1), (slab == 1) & (col == 0)
    half_rows = pn.cs // 2

    def taps(g):
        return pl.ds(3 * g, 3)

    def part_of(ref, g, half):
        return ref.at[taps(g), pl.ds(half * half_rows, half_rows)]

    def ship(g, half, up, src):
        to = slab + 1 if up else slab - 1
        return remote(part_of(src, g, half), part_of(wbuf, g, half), w_s.at[int(up), half, g], w_r.at[half, g],
                      (to * pn.G + x, col))

    def assist(g, up):
        to = slab + 1 if up else slab - 1
        return remote(part_of(w_in, g, 1), part_of(wbuf, g, 1), e_s.at[g], w_r.at[1, g], (to * pn.G + x, col + 2))

    def own_copy(g):
        return pltpu.make_async_copy(w_in.at[taps(g)], wbuf.at[taps(g)], w_l.at[g])

    def arrived(g):
        for half in (0, 1):
            at = part_of(wbuf, g, half)
            pltpu.make_async_copy(at, at, w_r.at[half, g]).wait()

    def pass_on(g):
        for role, up in ((rising, True), (falling, False)):
            @pl.when(role)
            def _(up=up):
                arrived(g)
                for half in (0, 1):
                    ship(g, half, up, wbuf).start()

    def w_wait(g):
        if pn.exchange:
            @pl.when(source)
            def _():
                own_copy(g).wait()

            @pl.when(jnp.logical_not(source | rising | falling))
            def _():
                arrived(g)
        else:
            own_copy(g).wait()

    def each_shipment(g, act):
        for half in (0, 1):
            @pl.when(source & ((slab < n - 2) if half else (slab < n - 1)))
            def _(half=half):
                act(ship(g, half, True, w_in))

            @pl.when(source & ((slab > 1) if half else (slab > 0)))
            def _(half=half):
                act(ship(g, half, False, w_in))

        @pl.when(help_up)
        def _():
            act(assist(g, True))

        @pl.when(help_down)
        def _():
            act(assist(g, False))

    if pn.exchange:
        def begin(g, carry):
            each_shipment(g, lambda c: c.start())

            @pl.when(source)
            def _():
                own_copy(g).start()

            return carry
    else:
        def begin(g, carry):
            own_copy(g).start()
            return carry

    lax.fori_loop(0, GROUPS, begin, 0)

    cot_sent = []
    for cc in range(1, pn.C):
        cd = lax.rem(col + cc, pn.C)
        c = remote(cot.at[pl.ds(cd * pn.rpb, pn.rpb)], cx.at[:, own_cols], c_s.at[cc], c_r.at[cc], (row, cd))
        c.start()
        cot_sent.append(c)
    cot_keep = pltpu.make_async_copy(cot.at[pl.ds(col * pn.rpb, pn.rpb)], cx.at[:, own_cols], c_r.at[0])
    cot_keep.start()

    def proj_row(k):
        return remote(proj.at[col], proj_out.at[col, row], j_s.at[k], j_r.at[k], (lax.rem(row + k, pn.R), col))

    def proj_col(k):
        return remote(proj_out.at[col], proj_out.at[col], t_s.at[k], t_r.at[k], (row, lax.rem(col + k, pn.C)))

    def proj_begin(k, carry):
        proj_row(k).start()
        return carry

    def proj_wait(k, carry):
        proj_row(k).wait()
        return carry

    lax.fori_loop(1, pn.R, proj_begin, 0)
    proj_keep = pltpu.make_async_copy(proj.at[col], proj_out.at[col, row], j_r.at[0])
    proj_keep.start()

    @pl.when(slab == 0)
    def _():
        ring[pl.ds(0, MARGIN)] = jnp.zeros((MARGIN, pn.C * bp, pn.cs), BF16)

    @pl.when(slab == n - 1)
    def _():
        ring[pl.ds(MARGIN + H, MARGIN)] = jnp.zeros((MARGIN, pn.C * bp, pn.cs), BF16)

    for c in sent:
        c.wait()
    keep.wait()

    def margin_down():
        return remote(ring.at[pl.ds(MARGIN, MARGIN)], ring.at[pl.ds(MARGIN + H, MARGIN)], h_s.at[0], h_r.at[0],
                      member(slab - 1, me))

    def margin_up():
        return remote(ring.at[pl.ds(H, MARGIN)], ring.at[pl.ds(0, MARGIN)], h_s.at[1], h_r.at[1], member(slab + 1, me))

    @pl.when(slab > 0)
    def _():
        margin_down().start()

    @pl.when(slab < n - 1)
    def _():
        margin_up().start()

    def pass_many(first, end):
        def one(g, carry):
            pass_on(g)
            return carry

        if pn.exchange:
            lax.fori_loop(first, end, one, 0)

    pass_many(0, 3)

    def assemble(rp, carry):
        pair = ring[pl.ds(2 * rp, 2)].reshape(2 * pn.C * bp, pn.cs)
        moved = dot(sel[...], pair).astype(BF16)
        at = pl.multiple_of(rp * 2 * pn.S, 16)
        for v in range(7):
            xs[v, pl.ds(at, 2 * pn.S)] = moved[v * 2 * pn.S:(v + 1) * 2 * pn.S]
        return carry

    lax.fori_loop(MARGIN // 2, (MARGIN + H) // 2, assemble, 0, unroll=6)
    for c in cot_sent:
        c.wait()
    cot_keep.wait()
    for rp in range(pn.rpb // 2):
        pair = cx[2 * rp:2 * rp + 2].reshape(2 * pn.C * bp, pn.width)
        cot_out[pl.ds(rp * 2 * pn.S, 2 * pn.S)] = dot(sel[pl.ds(3 * 2 * pn.S, 2 * pn.S)], pair).astype(BF16)
    lax.fori_loop(1, pn.R, proj_wait, 0)
    proj_keep.wait()
    for k in range(1, pn.C):
        proj_col(k).start()
    pass_many(3, 5)

    @pl.when(slab > 0)
    def _():
        margin_down().wait_send()
        margin_up().wait_recv()

    @pl.when(slab < n - 1)
    def _():
        margin_up().wait_send()
        margin_down().wait_recv()

    lax.fori_loop(0, MARGIN // 2, assemble, 0, unroll=3)
    lax.fori_loop((MARGIN + H) // 2, pn.nb * pn.rpb // 2, assemble, 0, unroll=3)
    x_save = pltpu.make_async_copy(xs, x_out, o_s.at[0])
    x_save.start()

    def first_stage(slot):
        return remote(pbuf.at[slot, :, 1 - core], cbuf.at[slot], r1_s.at[slot], r1_r.at[slot], (row, col + 1 - 2 * core))

    def second_stage(slot, i):
        q = lax.rem(quad + i, MEMBERS // 2)
        return remote(sbuf.at[slot, i - 1], rbuf.at[slot, i - 1], r2_s.at[slot, i - 1], r2_r.at[slot, i - 1],
                      member(slab, 2 * q + core))

    def middle(slot):
        first_stage(slot).wait()
        for i in (1, 2, 3, 0):
            q = lax.rem(quad + i, MEMBERS // 2)
            s = pbuf[slot, q, core].astype(F32) + cbuf[slot, q].astype(F32)
            if i == 0:
                p_out[slot] = s
            else:
                sbuf[slot, i - 1] = s.astype(BF16)
                second_stage(slot, i).start()

    def last(slot):
        total = p_out[slot]
        for i in range(1, MEMBERS // 2):
            second_stage(slot, i).wait()
            total = total + rbuf[slot, i - 1].astype(F32)
        p_out[slot] = total

    def scatter(slot, rb, y):
        for r in range(many):
            pbuf[slot, (many * rb + r) // 2, r % 2] = y[r * px:(r + 1) * px].astype(BF16)

    def far(g):
        if g + 5 < GROUPS:
            pass_many(g + 5, g + 6)
        w_wait(g)

    for branch in (1, 2, 3):
        step = pn.steps[branch - 1]
        for i in (-1, 0, 1):
            g = 3 * (branch - 1) + i + 1
            mask_at = (2 * (branch - 1) + (i + 1) // 2) * H
            far(g)

            def block(rb, carry, step=step, i=i, g=g, mask_at=mask_at, branch=branch):
                at = pl.multiple_of(rb * many * px, 16)
                window = pl.ds(pl.multiple_of((rb * many + pn.hb + i * step) * px, 16), many * px)
                y = dot(xs[3 - branch, window], wbuf[3 * g])
                y = y + dot(xs[3, window], wbuf[3 * g + 1])
                y = y + dot(xs[3 + branch, window], wbuf[3 * g + 2])
                if i != 0:
                    y = jnp.concatenate(
                        [y[r * pn.S:(r + 1) * pn.S] * masks[mask_at + rb * many * pn.rpb + r]
                         for r in range(many * pn.rpb)], axis=0
                    )
                if i > -1:
                    y = y + acc[pl.ds(at, many * px)]
                if i < 1:
                    acc[pl.ds(at, many * px)] = y
                else:
                    scatter(branch, rb, y)
                return carry

            lax.fori_loop(0, MEMBERS // many, block, 0)
            if i == 0 and branch > 1:
                middle(branch - 1)
        first_stage(branch).start()

    far(GROUPS - 1)

    def point(rb, carry):
        at = pl.ds(pl.multiple_of((rb * many + pn.hb) * px, 16), many * px)
        scatter(0, rb, dot(xs[3, at], wbuf[POINT]))
        return carry

    lax.fori_loop(0, MEMBERS // many, point, 0)
    first_stage(0).start()
    middle(3)

    sums = dot(hot_t[...], xs[3, pl.ds(pn.hb * px, pn.own)])
    means = sums * inv_counts[...]
    m_out[...] = means
    p4_out[...] = split_dot(dot, means, wbuf[POOL])
    w_save = pltpu.make_async_copy(wbuf, w_out, o_s.at[1])
    w_save.start()
    middle(0)
    for slot in (1, 2, 3):
        last(slot)
    for k in range(1, pn.C):
        proj_col(k).wait()
    if pn.exchange:
        def settled(g, carry):
            each_shipment(g, lambda c: c.wait_send())
            for role, up in ((rising, True), (falling, False)):
                @pl.when(role)
                def _(up=up):
                    for half in (0, 1):
                        ship(g, half, up, wbuf).wait_send()
            return carry

        lax.fori_loop(0, GROUPS, settled, 0)
    last(0)
    x_save.wait()
    w_save.wait()


def conv_forward(pn, feats, w, cot, proj, masks, sel, hot_t, inv_counts):
    half = MEMBERS // 2
    dma = pltpu.SemaphoreType.DMA
    vmem = pl.BlockSpec(memory_space=pltpu.VMEM)
    hbm = pl.BlockSpec(memory_space=pl.ANY)
    shape = jax.ShapeDtypeStruct
    return pl.pallas_call(
        functools.partial(conv_kernel, pn),
        out_shape=(
            shape((4, pn.px, pn.width), F32),
            shape((7, pn.ext, pn.cs), BF16),
            shape((TAPS, pn.cs, pn.width), BF16),
            shape((pn.ncp, pn.cs), F32),
            shape((pn.ncp, pn.width), F32),
            shape((pn.px, pn.width), BF16),
            shape((pn.C, pn.R, pn.piece, pn.width), BF16),
        ),
        in_specs=[hbm, hbm, hbm, hbm, pl.BlockSpec(memory_space=pltpu.SMEM), vmem, vmem, vmem],
        out_specs=(vmem, hbm, hbm, vmem, vmem, vmem, vmem),
        scratch_shapes=[
            pltpu.VMEM((pn.nb * pn.rpb, pn.C * pn.bp, pn.cs), BF16),
            pltpu.VMEM((7, pn.ext, pn.cs), BF16),
            pltpu.VMEM((TAPS, pn.cs, pn.width), BF16),
            pltpu.VMEM((pn.own, pn.width), F32),
            pltpu.VMEM((4, half, 2, pn.px, pn.width), BF16),
            pltpu.VMEM((4, half, pn.px, pn.width), BF16),
            pltpu.VMEM((4, half - 1, pn.px, pn.width), BF16),
            pltpu.VMEM((4, half - 1, pn.px, pn.width), BF16),
            pltpu.VMEM((pn.rpb, pn.C * pn.bp, pn.width), BF16),
            dma((MEMBERS,)), dma((MEMBERS,)), dma((2,)), dma((2,)), dma((pn.C,)), dma((pn.C,)),
            dma((pn.R,)), dma((pn.R,)), dma((pn.C,)), dma((pn.C,)),
            dma((2, 2, GROUPS)), dma((2, GROUPS)), dma((GROUPS,)), dma((GROUPS,)),
            dma((4,)), dma((4,)), dma((4, 3)), dma((4, 3)), dma((2,)),
        ],
        compiler_params=pltpu.CompilerParams(collective_id=0, has_side_effects=True, vmem_limit_bytes=60 * 2**20),
        name="conv_forward",
    )(feats, w, cot, proj, masks, sel, hot_t, inv_counts)


def norm_kernel(pn, p, p4_in, gains, biases, valid, pixels, w_proj, cot, hot, hot_t, sel_t,
                q_out, q4_out, dproj_out, res_out, dg_out, db_out,
                norm, slope, hbuf, gact, dh4, rx,
                a1, b1, a2, b2, a3, b3, a4, b4, as_s, as_r, bs_s, bs_r, e_s, e_r):
    row, col = lax.axis_index("row"), lax.axis_index("col")
    slab, x = row // pn.G, lax.rem(row, pn.G)
    me = x * pn.C + col
    crops = float(pn.crops)
    v = valid[...]
    inv_px = pixels[0]
    width, bp = pn.width, pn.bp

    def member(s, k):
        return (s * pn.G + k // pn.C, lax.rem(k, pn.C))

    barrier = pltpu.get_barrier_semaphore()
    for kk in range(1, MEMBERS):
        pl.semaphore_signal(barrier, inc=1, device_id=member(slab, lax.rem(me + kk, MEMBERS)), device_id_type=MESH)

    def hello(k, carry):
        pl.semaphore_signal(barrier, inc=1, device_id=member(lax.rem(slab + k, pn.slabs), me), device_id_type=MESH)
        return carry

    lax.fori_loop(1, pn.slabs, hello, 0)

    def peer_a(n, abuf, kk):
        return remote(abuf.at[me], abuf.at[me], as_s.at[n, kk], as_r.at[n, kk], member(slab, lax.rem(me + kk, MEMBERS)))

    def peer_b(n, bbuf, k):
        return remote(bbuf.at[slab], bbuf.at[slab], bs_s.at[n, k], bs_r.at[n, k], member(lax.rem(slab + k, pn.slabs), me))

    def reduce_start(n, abuf):
        for kk in range(1, MEMBERS):
            peer_a(n, abuf, kk).start()

    def reduce_end(n, abuf, bbuf):
        for kk in range(1, MEMBERS):
            peer_a(n, abuf, kk).wait()
        total = abuf[0]
        for k in range(1, MEMBERS):
            total = total + abuf[k]
        bbuf[slab] = total
        for k in range(1, pn.slabs):
            peer_b(n, bbuf, k).start()
        for k in range(1, pn.slabs):
            peer_b(n, bbuf, k).wait()
        total = bbuf[0]
        for k in range(1, pn.slabs):
            total = total + bbuf[k]
        return total

    def column_sum(value):
        return jnp.sum(value, axis=0, keepdims=True)

    for b in range(4):
        pv = p[b] * v
        a1[me, pl.ds(b, 1)] = column_sum(pv)
        a1[me, pl.ds(4 + b, 1)] = column_sum(pv * p[b])
    a1[me, pl.ds(8, pn.ncp)] = p4_in[...]
    pl.semaphore_wait(barrier, MEMBERS - 1 + pn.slabs - 1)
    reduce_start(0, a1)
    total = reduce_end(0, a1, b1)
    inv = []
    for b in range(4):
        centre = total[b:b + 1] * inv_px
        scale = lax.rsqrt(total[4 + b:5 + b] * inv_px - centre * centre + EPSILON)
        inv.append(scale)
        n = (p[b] - centre) * scale
        u = gains[b:b + 1] * n + biases[b:b + 1]
        s = jax.nn.sigmoid(u)
        norm[b] = n
        slope[b] = s * (1.0 + u * (1.0 - s))
        hbuf[b] = (u * s).astype(BF16)
    p4 = total[8:8 + pn.ncp]
    centre4 = column_sum(p4) * (1.0 / crops)
    inv4 = lax.rsqrt(column_sum(p4 * p4) * (1.0 / crops) - centre4 * centre4 + EPSILON)
    n4 = (p4 - centre4) * inv4
    u4 = gains[4:5] * n4 + biases[4:5]
    s4 = jax.nn.sigmoid(u4)
    slope4 = s4 * (1.0 + u4 * (1.0 - s4))
    hbuf[4] = dot(hot[...], (u4 * s4).astype(BF16)).astype(BF16)

    p5 = dot(hbuf[0], w_proj[pl.ds(0, width)])
    for b in range(1, 5):
        p5 = p5 + dot(hbuf[b], w_proj[pl.ds(b * width, width)])
    pv = p5 * v
    a2[me, pl.ds(0, 1)] = column_sum(pv)
    a2[me, pl.ds(1, 1)] = column_sum(pv * p5)
    a2[me, pl.ds(2, 6)] = jnp.zeros((6, width), F32)
    reduce_start(1, a2)
    total = reduce_end(1, a2, b2)
    centre5 = total[0:1] * inv_px
    inv5 = lax.rsqrt(total[1:2] * inv_px - centre5 * centre5 + EPSILON)
    n5 = (p5 - centre5) * inv5
    u5 = gains[5:6] * n5 + biases[5:6]
    s5 = jax.nn.sigmoid(u5)
    g5 = cot[...].astype(F32) * v * (s5 * (1.0 + u5 * (1.0 - s5)))
    norm[4] = n5
    gact[4] = g5
    a3[me, pl.ds(0, 1)] = column_sum(g5)
    a3[me, pl.ds(1, 1)] = column_sum(g5 * n5)
    a3[me, pl.ds(2, 6)] = jnp.zeros((6, width), F32)
    reduce_start(2, a3)
    hbuf[5] = (v * u5 * s5).astype(BF16)
    for rp in range(pn.rpb // 2):
        pair = hbuf[5, pl.ds(rp * 2 * pn.S, 2 * pn.S)]
        rx[2 * rp:2 * rp + 2] = dot(sel_t[...], pair).astype(BF16).reshape(2, pn.C * bp, width)
    back = []
    for cc in range(1, pn.C):
        cd = lax.rem(col + cc, pn.C)
        c = remote(rx.at[:, pl.ds(pl.multiple_of(cd * bp, bp), bp)], res_out.at[pl.ds(col * pn.rpb, pn.rpb)],
                   e_s.at[cc], e_r.at[cc], (row, cd))
        c.start()
        back.append(c)
    c = pltpu.make_async_copy(rx.at[:, pl.ds(pl.multiple_of(col * bp, bp), bp)], res_out.at[pl.ds(col * pn.rpb, pn.rpb)],
                              e_r.at[0])
    c.start()
    back.append(c)
    total = reduce_end(2, a3, b3)
    db5, dg5 = total[0:1], total[1:2]
    q5 = (gains[5:6] * inv5 * (gact[4] - v * (db5 + norm[4] * dg5) * inv_px)).astype(BF16)
    hbuf[5] = q5

    for b in range(4):
        g = dot_nt(q5, w_proj[pl.ds(b * width, width)]) * slope[b]
        gact[b] = g
        a4[me, pl.ds(b, 1)] = column_sum(g)
        a4[me, pl.ds(4 + b, 1)] = column_sum(g * norm[b])
    dh4[...] = dot_nt(q5, w_proj[pl.ds(4 * width, width)])
    high = dh4[...].astype(BF16)
    low = (dh4[...] - high.astype(F32)).astype(BF16)
    a4[me, pl.ds(8, pn.ncp)] = dot(hot_t[...], high) + dot(hot_t[...], low)
    reduce_start(3, a4)
    for b in range(5):
        dproj_out[pl.ds(b * width, width)] = dot_tn(hbuf[b], hbuf[5]).astype(BF16)
    total = reduce_end(3, a4, b4)
    for b in range(4):
        db, dg = total[b:b + 1], total[4 + b:5 + b]
        db_out[pl.ds(b, 1)] = db
        dg_out[pl.ds(b, 1)] = dg
        q_out[b] = (gains[b:b + 1] * inv[b] * (gact[b] - v * (db + norm[b] * dg) * inv_px)).astype(BF16)
    g4 = total[8:8 + pn.ncp] * slope4
    db4, dg4 = column_sum(g4), column_sum(g4 * n4)
    db_out[pl.ds(4, 1)] = db4
    dg_out[pl.ds(4, 1)] = dg4
    db_out[pl.ds(5, 1)] = db5
    dg_out[pl.ds(5, 1)] = dg5
    q4_out[...] = (gains[4:5] * inv4 * (g4 - (db4 + n4 * dg4) * (1.0 / crops))).astype(BF16)
    for c in back:
        c.wait()


def norms(pn, p, p4, gains, biases, valid, pixels, w_proj, cot, hot, hot_t, sel_t):
    dma = pltpu.SemaphoreType.DMA
    vmem = pl.BlockSpec(memory_space=pltpu.VMEM)
    shape = jax.ShapeDtypeStruct
    big, small = 8 + pn.ncp, 8
    bufs = []
    for n in (big, small, small, big):
        bufs += [pltpu.VMEM((MEMBERS, n, pn.width), F32), pltpu.VMEM((pn.slabs, n, pn.width), F32)]
    return pl.pallas_call(
        functools.partial(norm_kernel, pn),
        out_shape=(
            shape((4, pn.px, pn.width), BF16),
            shape((pn.ncp, pn.width), BF16),
            shape((5 * pn.width, pn.width), BF16),
            shape((pn.h, pn.bp, pn.width), BF16),
            shape((6, pn.width), F32),
            shape((6, pn.width), F32),
        ),
        in_specs=[vmem] * 5 + [pl.BlockSpec(memory_space=pltpu.SMEM)] + [vmem] * 5,
        out_specs=(vmem,) * 6,
        scratch_shapes=[
            pltpu.VMEM((5, pn.px, pn.width), F32),
            pltpu.VMEM((4, pn.px, pn.width), F32),
            pltpu.VMEM((6, pn.px, pn.width), BF16),
            pltpu.VMEM((5, pn.px, pn.width), F32),
            pltpu.VMEM((pn.px, pn.width), F32),
            pltpu.VMEM((pn.rpb, pn.C * pn.bp, pn.width), BF16),
            *bufs,
            dma((4, MEMBERS)), dma((4, MEMBERS)), dma((4, pn.slabs)), dma((4, pn.slabs)), dma((pn.C,)), dma((pn.C,)),
        ],
        compiler_params=pltpu.CompilerParams(collective_id=1, has_side_effects=True, vmem_limit_bytes=48 * 2**20),
        name="norms",
    )(p, p4, gains, biases, valid, pixels, w_proj, cot, hot, hot_t, sel_t)


BACK = tuple((b, i) for b in (1, 2, 3) for i in (-1, 1)) + tuple((b, 0) for b in (1, 2, 3))


def group_of(k):
    middle = k // 6
    return (1 - middle) * (3 * (k // 2) + 2 * (k % 2)) + middle * jnp.minimum(1 + 3 * (k - 6), GROUPS - 1)


def back_kernel(pn, q_in, x_in, w_in, dproj_in, q4, means, hot_px, inv_counts, masks, lane_masks, shifts, sel_t,
                dw_out, dx_out, dproj_out,
                xs, wbuf, qraw, qs, qt, dxe, dwbuf, inn, hsend, hrecv, pack, dp1, dps, dp2, dpf,
                l_s, q_s, q_r, k_s, k_r, f_s, f_r, n_s, n_r, e_s, e_r, g_s, g_r, h_s, h_r, x_s, x_r,
                p1_s, p1_r, p2_s, p2_r, p3_s, p3_r):
    row, col = lax.axis_index("row"), lax.axis_index("col")
    slab, x = row // pn.G, lax.rem(row, pn.G)
    me = x * pn.C + col
    core, quad = lax.rem(col, 2), me // 2
    h, H, bp, px, S, n = pn.h, pn.H, pn.bp, pn.px, pn.S, pn.slabs
    half = MEMBERS // 2
    many = 4
    partner = (row, col + 1 - 2 * core)

    def member(s, k):
        return (s * pn.G + k // pn.C, lax.rem(k, pn.C))

    load_x = pltpu.make_async_copy(x_in, xs, l_s.at[0])
    load_w = pltpu.make_async_copy(w_in, wbuf, l_s.at[1])
    load_x.start()
    load_w.start()
    greet_all(pn, row, col)

    own_px = pl.ds(pl.multiple_of(me * px, 16), px)
    along_y, along_x = (row, lax.rem(col + 2, pn.C)), (slab * pn.G + lax.rem(x + 1, pn.G), col)
    from_y = x * pn.C + lax.rem(col + 2, pn.C)
    from_x = lax.rem(me + pn.C, MEMBERS)
    from_xy = lax.rem(from_y + pn.C, MEMBERS)

    def block_of(slot, k):
        return qraw.at[slot, pl.ds(pl.multiple_of(k * px, 16), px)]

    def to_y(slot):
        return remote(q_in.at[slot], qraw.at[slot, own_px], q_s.at[slot, 0], q_r.at[slot, 0], along_y)

    def to_x(slot):
        return remote(q_in.at[slot], qraw.at[slot, own_px], q_s.at[slot, 1], q_r.at[slot, 1], along_x)

    def on_to_x(slot):
        return remote(block_of(slot, from_y), block_of(slot, from_y), q_s.at[slot, 2], q_r.at[slot, 2], along_x)

    def to_partner(slot):
        return remote(q_in.at[slot], qraw.at[slot, own_px], k_s.at[slot], k_r.at[slot], partner)

    def passed(slot, i):
        at = block_of(slot, (from_y, from_x, from_xy)[i])
        return remote(at, at, f_s.at[slot, i], f_r.at[slot, i], partner)

    def kept(slot):
        return pltpu.make_async_copy(q_in.at[slot], qraw.at[slot, own_px], l_s.at[2 + slot])

    slots = (1, 2, 3, 0)
    for slot in slots:
        to_y(slot).start()
        to_x(slot).start()
        to_partner(slot).start()
        kept(slot).start()

    block_rows = 5 * pn.width // MEMBERS
    home_slab = me // pn.G

    def dproj_slab(kk):
        other = lax.rem(me + kk, MEMBERS)
        return remote(dproj_in.at[pl.ds(pl.multiple_of(other * block_rows, 16), block_rows)], dp1.at[me],
                      p1_s.at[kk], p1_r.at[kk], member(slab, other))

    def dproj_own():
        return pltpu.make_async_copy(dproj_in.at[pl.ds(pl.multiple_of(me * block_rows, 16), block_rows)], dp1.at[me],
                                     p1_r.at[0])

    def dproj_home():
        return remote(dps, dp2.at[slab], p2_s.at[0], p2_r.at[slab], member(home_slab, me))

    def dproj_give(c):
        return remote(dpf, dproj_out, p3_s.at[c], p3_r.at[0], (slab * pn.G + lax.rem(me, pn.G), c))

    if pn.exchange:
        for kk in range(1, MEMBERS):
            dproj_slab(kk).start()
        dproj_own().start()

    def clear(rb, carry):
        dxe[pl.ds(pl.multiple_of(rb * px, 16), px)] = jnp.zeros((px, pn.cs), F32)
        return carry

    lax.fori_loop(0, pn.nb, clear, 0)

    def receive_y(slot):
        to_y(slot).wait()
        on_to_x(slot).start()
        passed(slot, 0).start()

    def receive_x(slot):
        to_x(slot).wait()
        passed(slot, 1).start()
        on_to_x(slot).wait()
        passed(slot, 2).start()

    def received(slot):
        to_partner(slot).wait()
        kept(slot).wait()
        for i in range(3):
            passed(slot, i).wait()

    home = home_of(pn, col)
    closing, rising, falling = slab == home, slab < home, slab > home
    first = (slab == 0) | (slab == n - 1)
    half_rows = pn.cs // 2
    detour_up, detour_down = (slab == 0) & (col == 2), (slab == n - 1) & (col == 3)
    relay_up, relay_down = (slab == 0) & (col == 0), (slab == n - 1) & (col == 1)

    def taps(g):
        return pl.ds(3 * g, 3)

    def part_of(ref, g, half):
        return ref.at[taps(g), pl.ds(half * half_rows, half_rows)]

    def link(g, half, up):
        side, to = (0, slab + 1) if up else (1, slab - 1)
        return remote(part_of(dwbuf, g, half), part_of(inn.at[side], g, half), n_s.at[half, g], n_r.at[side, half, g],
                      (to * pn.G + x, col))

    def detour(g, up):
        side = 0 if up else 1
        return remote(part_of(dwbuf, g, 1), part_of(inn.at[side], g, 1), n_s.at[1, g], e_r.at[g], (row, col - 2))

    def relay(g, up):
        side, to = (0, slab + 1) if up else (1, slab - 1)
        return remote(part_of(inn.at[side], g, 1), part_of(inn.at[side], g, 1), e_s.at[g], n_r.at[side, 1, g],
                      (to * pn.G + x, col + 2))

    def each_link(g, act):
        for going, up, around in ((rising, True, detour_up), (falling, False, detour_down)):
            @pl.when(going)
            def _(up=up):
                act(link(g, 0, up))

            @pl.when(going & jnp.logical_not(around))
            def _(up=up):
                act(link(g, 1, up))

            @pl.when(around)
            def _(up=up):
                act(detour(g, up))

    def arrived(g, side):
        for half in (0, 1):
            at = part_of(inn.at[side], g, half)
            pltpu.make_async_copy(at, at, n_r.at[side, half, g]).wait()

    def add(g, side):
        dwbuf[taps(g)] = (dwbuf[taps(g)].astype(F32) + inn[side, taps(g)].astype(F32)).astype(BF16)

    def share_y(g):
        return remote(dwbuf.at[taps(g)], dw_out.at[taps(g)], g_s.at[0, g], g_r.at[g], (row, lax.rem(col + 2, pn.C)))

    def share_core(g):
        return remote(dwbuf.at[taps(g)], dw_out.at[taps(g)], g_s.at[1, g], g_r.at[g], partner)

    def share_on(g):
        return remote(dw_out.at[taps(g)], dw_out.at[taps(g)], g_s.at[0, g], g_r.at[g], partner)

    shared_on = home_of(pn, lax.rem(col + 2, pn.C)) == slab

    def landed(g):
        pltpu.make_async_copy(dw_out.at[taps(g)], dw_out.at[taps(g)], g_r.at[g]).wait()

    def serve(k, carry):
        g = group_of(k)
        for role, up in ((relay_up, True), (relay_down, False)):
            @pl.when(role)
            def _(up=up):
                side = 0 if up else 1
                at = part_of(inn.at[side], g, 1)
                pltpu.make_async_copy(at, at, e_r.at[g]).wait()
                relay(g, up).start()

        @pl.when(rising & jnp.logical_not(first))
        def _():
            arrived(g, 0)
            add(g, 0)
            for half in (0, 1):
                link(g, half, True).start()

        @pl.when(falling & jnp.logical_not(first))
        def _():
            arrived(g, 1)
            add(g, 1)
            for half in (0, 1):
                link(g, half, False).start()

        @pl.when(closing)
        def _():
            @pl.when(slab > 0)
            def _():
                arrived(g, 0)
                add(g, 0)

            @pl.when(slab < n - 1)
            def _():
                arrived(g, 1)
                add(g, 1)

            share_y(g).start()
            share_core(g).start()
            pltpu.make_async_copy(dwbuf.at[taps(g)], dw_out.at[taps(g)], g_r.at[g]).start()

        @pl.when(shared_on & (k > 1))
        def _():
            before = group_of(jnp.maximum(k - 2, 0))
            landed(before)
            share_on(before).start()

        return carry

    receive_y(1)
    receive_y(2)
    load_x.wait()
    load_w.wait()
    receive_x(1)
    receive_y(3)

    def start_group(k):
        if not pn.exchange:
            return
        g = group_index(k)

        @pl.when(first)
        def _():
            each_link(g, lambda c: c.start())

    def group_index(k):
        if k < len(BACK):
            b, i = BACK[k]
            return 3 * (b - 1) + i + 1
        return GROUPS - 1

    for k, (branch, i) in enumerate(BACK):
        step = pn.steps[branch - 1]
        g = group_index(k)
        if i == -1:
            received(branch)
            if branch == 2:
                receive_y(0)
            receive_x(branch + 1 if branch < 3 else 0)

            def turn(rp, carry, branch=branch):
                at = pl.multiple_of(rp * 2 * S, 16)
                moved = dot(shifts[pl.ds((branch - 1) * 4 * S, 4 * S)], qraw[branch, pl.ds(at, 2 * S)]).astype(BF16)
                qs[branch - 1, 0, pl.ds(at, 2 * S)] = moved[:2 * S]
                qs[branch - 1, 1, pl.ds(at, 2 * S)] = moved[2 * S:]
                return carry

            lax.fori_loop(0, H // 2, turn, 0, unroll=6)
        if i != 1:
            qt[...] = qraw[branch].T
        q_turned = qt[...]
        if i != 0:
            q_turned = q_turned * lane_masks[pl.ds(2 * (branch - 1) + (i + 1) // 2, 1)]
        window = pl.ds((pn.hb + i * step) * px, pn.own)
        for j in (-1, 0, 1):
            dwbuf[3 * g + j + 1] = dot(q_turned, xs[3 + j * branch, window]).T.astype(BF16)
        start_group(k)
        mask_at = (2 * (branch - 1) + (i + 1) // 2) * H

        def block(rb, carry, branch=branch, i=i, step=step, g=g, mask_at=mask_at):
            at = pl.ds(pl.multiple_of(rb * many * px, 16), many * px)
            y = dot_nt(qs[branch - 1, 0, at], wbuf[3 * g])
            y = y + dot_nt(qraw[branch, at], wbuf[3 * g + 1])
            y = y + dot_nt(qs[branch - 1, 1, at], wbuf[3 * g + 2])
            if i != 0:
                y = jnp.concatenate(
                    [y[r * S:(r + 1) * S] * masks[mask_at + rb * many * pn.rpb + r] for r in range(many * pn.rpb)], axis=0
                )
            to = pl.ds(pl.multiple_of((rb * many + pn.hb + i * step) * px, 16), many * px)
            dxe[to] = dxe[to] + y
            return carry

        lax.fori_loop(0, MEMBERS // many, block, 0)
        if k == 5:
            hsend[0] = dxe[pl.ds(0, pn.hb * px)].astype(BF16)
            hsend[1] = dxe[pl.ds((pn.hb + MEMBERS) * px, pn.hb * px)].astype(BF16)

            @pl.when(slab > 0)
            def _():
                remote(hsend.at[0], hrecv.at[1], h_s.at[0], h_r.at[1], member(slab - 1, me)).start()

            @pl.when(slab < n - 1)
            def _():
                remote(hsend.at[1], hrecv.at[0], h_s.at[1], h_r.at[0], member(slab + 1, me)).start()

        if pn.exchange and k == 3:
            for kk in range(1, MEMBERS):
                dproj_slab(kk).wait()
            dproj_own().wait()
            total = dp1[0].astype(F32)
            for m in range(1, MEMBERS):
                total = total + dp1[m].astype(F32)
            dps[...] = total.astype(BF16)

            @pl.when(slab != home_slab)
            def _():
                dproj_home().start()

            @pl.when(slab == home_slab)
            def _():
                pltpu.make_async_copy(dps, dp2.at[slab], p2_r.at[slab]).start()

    received(0)
    dwbuf[POOL] = dot_tn(means[...].astype(BF16), q4[...]).astype(BF16)
    dwbuf[POINT] = dot(qraw[0].T, xs[3, pl.ds(pn.hb * px, pn.own)]).T.astype(BF16)
    dwbuf[TAPS - 1] = jnp.zeros((pn.cs, pn.width), BF16)
    start_group(GROUPS - 1)
    pooled = dot_nt(q4[...], wbuf[POOL]) * inv_counts[...]
    pooled_high = pooled.astype(BF16)
    pooled_low = (pooled - pooled_high.astype(F32)).astype(BF16)

    def finish(rb, carry):
        at = pl.ds(pl.multiple_of(rb * many * px, 16), many * px)
        to = pl.ds(pl.multiple_of((rb * many + pn.hb) * px, 16), many * px)
        hot = hot_px[at]
        y = dot_nt(qraw[0, at], wbuf[POINT]) + dot(hot, pooled_high) + dot(hot, pooled_low)
        dxe[to] = dxe[to] + y
        return carry

    lax.fori_loop(0, MEMBERS // many, finish, 0)
    if pn.exchange:
        lax.fori_loop(0, 6, serve, 0)

        @pl.when(slab == home_slab)
        def _():
            for z in range(n):
                pltpu.make_async_copy(dp2.at[z], dp2.at[z], p2_r.at[z]).wait()
            total = dp2[0].astype(F32)
            for z in range(1, n):
                total = total + dp2[z].astype(F32)
            dpf[...] = total
            for c in range(pn.C):
                @pl.when((x == lax.rem(me, pn.G)) & (col == c))
                def _():
                    pltpu.make_async_copy(dpf, dproj_out, p3_r.at[0]).start()

                @pl.when(jnp.logical_not((x == lax.rem(me, pn.G)) & (col == c)))
                def _(c=c):
                    dproj_give(c).start()

    @pl.when(slab > 0)
    def _():
        remote(hsend.at[0], hrecv.at[1], h_s.at[0], h_r.at[1], member(slab - 1, me)).wait_send()
        remote(hsend.at[1], hrecv.at[0], h_s.at[1], h_r.at[0], member(slab - 1, me)).wait_recv()

    @pl.when(slab < n - 1)
    def _():
        remote(hsend.at[1], hrecv.at[0], h_s.at[1], h_r.at[0], member(slab + 1, me)).wait_send()
        remote(hsend.at[0], hrecv.at[1], h_s.at[0], h_r.at[1], member(slab + 1, me)).wait_recv()

    @pl.when(slab == 0)
    def _():
        hrecv[0] = jnp.zeros((pn.hb * px, pn.cs), BF16)

    @pl.when(slab == n - 1)
    def _():
        hrecv[1] = jnp.zeros((pn.hb * px, pn.cs), BF16)

    for rb in range(pn.hb):
        low, high = (pn.hb + rb) * px, (MEMBERS + rb) * px
        dxe[pl.ds(low, px)] = dxe[pl.ds(low, px)] + hrecv[0, pl.ds(rb * px, px)].astype(F32)
        dxe[pl.ds(high, px)] = dxe[pl.ds(high, px)] + hrecv[1, pl.ds(rb * px, px)].astype(F32)

    def packing(rp, carry):
        pair = dxe[pl.ds(pl.multiple_of(pn.hb * px + rp * 2 * S, 16), 2 * S)].astype(BF16)
        pack[pl.ds(2 * rp, 2)] = dot(sel_t[...], pair).astype(BF16).reshape(2, pn.C * bp, pn.cs)
        return carry

    lax.fori_loop(0, H // 2, packing, 0, unroll=6)
    back = []
    for kk in range(1, MEMBERS):
        other = lax.rem(me + kk, MEMBERS)
        xo, co = other // pn.C, lax.rem(other, pn.C)
        c = remote(pack.at[pl.ds(xo * h, h), pl.ds(pl.multiple_of(co * bp, bp), bp)], dx_out.at[slice_of(pn, me)], x_s.at[kk], x_r.at[kk],
                   member(slab, other))
        c.start()
        back.append(c)
    c = pltpu.make_async_copy(pack.at[pl.ds(x * h, h), pl.ds(pl.multiple_of(col * bp, bp), bp)], dx_out.at[slice_of(pn, me)], x_r.at[0])
    c.start()
    back.append(c)

    if pn.exchange:
        lax.fori_loop(6, GROUPS, serve, 0)

        @pl.when(shared_on)
        def _():
            for k in (GROUPS - 2, GROUPS - 1):
                landed(group_index(k))
                share_on(group_index(k)).start()

        def settle(g, carry):
            each_link(g, lambda c: c.wait_send())
            for role, up in ((relay_up, True), (relay_down, False)):
                @pl.when(role)
                def _(up=up):
                    relay(g, up).wait_send()

            @pl.when(closing)
            def _():
                share_y(g).wait_send()
                share_core(g).wait_send()

            @pl.when(shared_on)
            def _():
                share_on(g).wait_send()

            @pl.when(jnp.logical_not(shared_on))
            def _():
                landed(g)

            return carry

        lax.fori_loop(0, GROUPS, settle, 0)

        @pl.when(slab != home_slab)
        def _():
            dproj_home().wait_send()

        @pl.when(slab == home_slab)
        def _():
            for c in range(pn.C):
                @pl.when(jnp.logical_not((x == lax.rem(me, pn.G)) & (col == c)))
                def _(c=c):
                    dproj_give(c).wait_send()

        pltpu.make_async_copy(dproj_out, dproj_out, p3_r.at[0]).wait()
    else:
        c = pltpu.make_async_copy(dwbuf, dw_out, g_r.at[0])
        c.start()
        c.wait()
        dproj_out[...] = jnp.zeros(dproj_out.shape, F32)
    for c in back:
        c.wait()


def conv_backward(pn, q, xs, w, dproj, q4, means, hot_px, inv_counts, masks, lane_masks, shifts, sel_t):
    dma = pltpu.SemaphoreType.DMA
    vmem = pl.BlockSpec(memory_space=pltpu.VMEM)
    hbm = pl.BlockSpec(memory_space=pl.ANY)
    shape = jax.ShapeDtypeStruct
    n = pn.slabs if pn.exchange else 1
    sums = TAPS if pn.exchange else 1
    block_rows = 5 * pn.width // MEMBERS
    return pl.pallas_call(
        functools.partial(back_kernel, pn),
        out_shape=(
            shape((TAPS, pn.cs, pn.width), BF16),
            shape((MEMBERS, pn.h, pn.bp, pn.cs), BF16),
            shape((block_rows, pn.width), F32),
        ),
        in_specs=[hbm] * 4 + [vmem] * 4 + [pl.BlockSpec(memory_space=pltpu.SMEM)] + [vmem] * 3,
        out_specs=(hbm, hbm, vmem),
        scratch_shapes=[
            pltpu.VMEM((7, pn.ext, pn.cs), BF16),
            pltpu.VMEM((TAPS, pn.cs, pn.width), BF16),
            pltpu.VMEM((4, pn.own, pn.width), BF16),
            pltpu.VMEM((3, 2, pn.own, pn.width), BF16),
            pltpu.VMEM((pn.width, pn.own), BF16),
            pltpu.VMEM((pn.ext, pn.cs), F32),
            pltpu.VMEM((TAPS, pn.cs, pn.width), BF16),
            pltpu.VMEM((2, sums, pn.cs, pn.width), BF16),
            pltpu.VMEM((2, pn.hb * pn.px, pn.cs), BF16),
            pltpu.VMEM((2, pn.hb * pn.px, pn.cs), BF16),
            pltpu.VMEM((pn.H, pn.C * pn.bp, pn.cs), BF16),
            pltpu.VMEM((MEMBERS, block_rows, pn.width), BF16),
            pltpu.VMEM((block_rows, pn.width), BF16),
            pltpu.VMEM((n, block_rows, pn.width), BF16),
            pltpu.VMEM((block_rows, pn.width), F32),
            dma((6,)), dma((4, 3)), dma((4, 3)), dma((4,)), dma((4,)), dma((4, 3)), dma((4, 3)),
            dma((2, GROUPS)), dma((2, 2, GROUPS)), dma((GROUPS,)), dma((GROUPS,)), dma((2, GROUPS)), dma((GROUPS,)),
            dma((2,)), dma((2,)), dma((MEMBERS,)), dma((MEMBERS,)),
            dma((MEMBERS,)), dma((MEMBERS,)), dma((1,)), dma((n,)), dma((pn.C,)), dma((1,)),
        ],
        compiler_params=pltpu.CompilerParams(collective_id=2, has_side_effects=True, vmem_limit_bytes=61900 * 1024),
        name="conv_backward",
    )(q, xs, w, dproj, q4, means, hot_px, inv_counts, masks, lane_masks, shifts, sel_t)


def column_tables(pn):
    S, bp, bc = pn.S, pn.bp, pn.bc
    sel = np.zeros((7, 2, S, 2, pn.C * bp), np.float32)
    shifts = np.zeros((3, 2, 2, S, 2, S), np.float32)
    for r in range(2):
        for c in range(pn.cols):
            for v in range(-3, 4):
                s = c + v * DILATIONS[0]
                if 0 <= s < pn.cols:
                    sel[v + 3, r, c, r, (s // bc) * bp + s % bc] = 1.0
            for b, d in enumerate(DILATIONS):
                for n, j in enumerate((-1, 1)):
                    s = c - j * d
                    if 0 <= s < pn.cols:
                        shifts[b, n, r, c, r, s] = 1.0
    sel = sel.reshape(7 * 2 * S, 2 * pn.C * bp)
    sel_t = sel[3 * 2 * S:4 * 2 * S].T
    return (jnp.asarray(sel, BF16), jnp.asarray(sel_t, BF16), jnp.asarray(shifts.reshape(12 * S, 2 * S), BF16))


def per_device(
    features, crop_rows, crop_cols, w_point, w_atrous, w_pool, w_proj, gains, biases, cotangent
):
    h, bc, channels = features.shape
    pn = Plan(lax.axis_size("row"), lax.axis_size("col"), h, bc, channels, gains.shape[1], crop_rows.shape[0])
    row, col = lax.axis_index("row"), lax.axis_index("col")
    slab, x = row // pn.G, row % pn.G
    crop_ids = jnp.arange(pn.crops, dtype=jnp.int32)
    ends = jnp.cumsum(crop_rows)
    counts = (crop_rows * crop_cols).astype(F32)
    pixels = jnp.sum(counts)

    def crop_of(rows):
        found = jnp.sum((rows[:, None] >= ends[None, :]).astype(jnp.int32), axis=1)
        return jnp.where(rows < 0, -1, found)

    def widths_of(crop):
        return jnp.sum(jnp.where(crop[:, None] == crop_ids[None, :], crop_cols[None, :], 0), axis=1)

    own_crop = crop_of(row * h + jnp.arange(h, dtype=jnp.int32))
    own_columns = col * bc + jnp.arange(bc, dtype=jnp.int32)
    own_valid = own_columns[None, :] < widths_of(own_crop)[:, None]
    masked = jnp.where(own_valid[:, :, None], features, 0)
    feats = masked.reshape(h, bc, MEMBERS, pn.cs).transpose(2, 0, 1, 3)
    feats = jnp.pad(feats, ((0, 0), (0, 0), (0, pn.bp - bc), (0, 0)))
    cot = jnp.pad(cotangent, ((0, 0), (0, pn.bp - bc), (0, 0)))

    slab_rows = slab * pn.H - MARGIN + jnp.arange(pn.H + 2 * MARGIN, dtype=jnp.int32)
    crops = crop_of(slab_rows)
    mid = crops[MARGIN:MARGIN + pn.H]
    same = jnp.stack(
        [crops[MARGIN + i * d:MARGIN + i * d + pn.H] == mid for d in DILATIONS for i in (-1, 1)]
    ).astype(F32)
    lane_masks = jnp.pad(jnp.repeat(same, pn.S, axis=1), ((0, 2), (0, 0))).astype(BF16)
    ncp_ids = jnp.arange(pn.ncp, dtype=jnp.int32)
    hot_rows = (mid[:, None] == ncp_ids[None, :]).astype(BF16)
    hot_px = jnp.repeat(hot_rows, pn.S, axis=0)
    hot_t = jnp.repeat(hot_rows.T, pn.S, axis=1)
    inv_counts = jnp.pad(1.0 / counts, (0, pn.ncp - pn.crops))[:, None]

    k = x * pn.C + col
    block_crop = lax.dynamic_slice_in_dim(mid, k * pn.rpb, pn.rpb)
    columns = jnp.arange(pn.S, dtype=jnp.int32)
    valid = (columns[None, :] < widths_of(block_crop)[:, None]).astype(F32).reshape(pn.px, 1)
    block_hot = jnp.repeat((block_crop[:, None] == ncp_ids[None, :]).astype(BF16), pn.S, axis=0)
    block_hot_t = jnp.repeat((ncp_ids[:, None] == block_crop[None, :]).astype(BF16), pn.S, axis=1)

    sel, sel_t, shifts = column_tables(pn)
    none = jnp.zeros((1, *w_point.shape), BF16)
    w = jnp.concatenate([w_atrous.transpose(1, 0, 2), w_point[None], w_pool[None], none], axis=0)
    proj = w_proj.reshape(pn.C, pn.proj // pn.C, pn.width)
    proj = jnp.pad(proj, ((0, 0), (0, pn.piece - pn.proj // pn.C), (0, 0)))
    if not pn.exchange:
        w = lax.all_gather(w, "row", axis=1, tiled=True)
        w = lax.dynamic_slice_in_dim(w, slice_of(pn, x * pn.C + col) * pn.cs, pn.cs, axis=1)
    flat = same.reshape(-1)
    p, xs, w_own, means, p4, own_cot, pieces = conv_forward(pn, feats, w, cot, proj, flat, sel, hot_t, inv_counts)
    full_proj = pieces[:, :, :pn.proj // pn.C].transpose(1, 0, 2, 3).reshape(5 * pn.width, pn.width)
    q, q4, d_proj, res, d_gains, d_biases = norms(
        pn, p, p4, gains, biases, valid, (1.0 / pixels)[None], full_proj, own_cot, block_hot, block_hot_t, sel_t
    )
    dw, dx, dproj_sum = conv_backward(
        pn, q, xs, w_own, d_proj, q4, means, hot_px, inv_counts, flat, lane_masks, shifts, sel_t
    )
    if pn.exchange:
        d_proj = dproj_sum
    else:
        whole = jnp.zeros((TAPS, channels, pn.width), BF16)
        whole = lax.dynamic_update_slice(whole, dw, (0, slice_of(pn, x * pn.C + col) * pn.cs, 0))
        whole = lax.psum(whole, "col")
        dw = lax.psum_scatter(whole, "row", scatter_dimension=1, tiled=True)
        d_proj = lax.psum(d_proj, "col")
        d_proj = lax.psum_scatter(d_proj.astype(F32), "row", scatter_dimension=0, tiled=True)
    result = res[:, :bc]
    dx = dx[:, :, :bc].transpose(1, 2, 0, 3).reshape(h, bc, channels)
    d_features = jnp.where(own_valid[:, :, None], dx, 0)
    d_point = dw[POINT].astype(F32)
    d_atrous = dw[:POINT].astype(F32).transpose(1, 0, 2)
    d_pool = dw[POOL].astype(F32)
    return (result, d_features, d_point, d_atrous, d_pool, d_proj, d_gains, d_biases)


def solution(mesh):
    return jax.shard_map(
        per_device,
        mesh=mesh,
        in_specs=(
            P("row", "col", None),
            P(),
            P(),
            P("row", None),
            P("row", None, None),
            P("row", None),
            P("row", None),
            P(),
            P(),
            P("row", "col", None),
        ),
        out_specs=(
            P("row", "col", None),
            P("row", "col", None),
            P("row", None),
            P("row", None, None),
            P("row", None),
            P("row", None),
            P(),
            P(),
        ),
        check_vma=False,
    )
```

profile of v0, /device:TPU:9, one launch (start us, length us, event | category | flops | bytes accessed | tf_op | source)
XLA Modules:
  0.0 354.7 jit_solution(15026173396849627569)
XLA Ops:
  0.7 0.8 reduce-window.8
  1.5 0.1 convert_reduce_fusion
  1.6 0.1 compare_bitcast_fusion
  1.7 0.7 reshape.166.masks
  2.5 0.2 broadcast_in_dim.109
  2.6 0.9 reshape.159.hot_t
  3.5 0.1 convert_reduce_fusion.1
  3.6 0.7 select_reduce_fusion.1
  4.3 0.1 broadcast_compare_fusion
  4.4 1.5 broadcast_select_fusion.1
  5.9 0.4 copy.42
  6.3 0.8 copy.44
  7.1 1.4 pad.21.feats
  8.4 0.6 convert_reduce_fusion.2
  9.0 0.7 copy.36.inv_counts
  9.7 0.1 pad.29.clone
  9.8 3.1 maximum_maximum_fusion.w_in
  13.0 0.7 pad.22.cot
  13.7 0.6 pad.23.proj
  14.3 122.8 %conv_forward.1 = (f32[4,336,256]{2,1,0:T(8,128)}, bf16[7,4704,256]{2,1,0:T(8,128)(2,1)}, bf16[30,256,256]{2,1,0:T(8,128)(2,1)}, f32[16,256]{1,0:T(8,128)}, f32[...) custom-call(bf16[8,24,16,256]{3,2,1,0:T(8,128)(2,1)} %pad.21.feats, ...), custom_call_target="tpu_custom_call" | custom-call | tf_op jit(solution)/shard_map/conv_forward/pallas_call | solution.py:421
  137.2 1.2 slice_bitcast_fusion.1
  138.5 0.1 dynamic_slice.3
  138.6 0.2 select_reduce_fusion
  138.8 0.1 fusion.3
  138.8 0.1 reshape.170.valid
  139.0 0.1 fusion.4
  139.1 0.1 broadcast_in_dim.115
  139.2 0.1 reshape.162.hot_t
  140.0 36.2 %norms.1 = (bf16[4,336,256]{2,1,0:T(8,128)(2,1)S(1)}, bf16[16,256]{1,0:T(8,128)(2,1)S(1)}, bf16[1280,256]{1,0:T(8,128)(2,1)S(1)}, bf16[24,16,256]{2,1,0:T(8,128)...) custom-call(f32[4,336,256]{2,1,0:T(8,128)S(1)} %copy-done, f32[16,256]{1,0:T(8,128)S(1)} %copy-done.5, ...), custom_call_target="tpu_custom_call" | custom-call | tf_op jit(solution)/shard_map/norms/pallas_call | solution.py:614
  176.3 0.8 copy-done.1
  177.1 0.8 copy-done.2
  178.0 0.6 copy-done.8
  178.5 0.1 broadcast_in_dim.117
  178.7 0.2 reshape.164
  178.8 0.6 pad.25.lane_masks
  179.4 0.1 fusion
  179.5 0.9 broadcast_in_dim.116
  180.5 158.2 %conv_backward.1 = (bf16[30,256,256]{2,1,0:T(8,128)(2,1)}, bf16[8,24,16,256]{3,2,1,0:T(8,128)(2,1)}, f32[160,256]{1,0:T(8,128)}) custom-call(bf16[4,336,256]{2,1,0:T(8,128)(2,1)} %copy-done.1, bf16[7,4704,256]{2,1,0:T(8,128)(2,1)} %get-tuple-element.30.x_in, bf16[30,256,256]{2,1,0:T(8,128)(2,1)} %get-tuple-element.31.w_in, bf16[1280,256]{1,0:T(8,128)(2,1)} %copy-done.2, ...), custom_call_target="tpu_custom_call" | custom-call | tf_op jit(solution)/shard_map/conv_backward/pallas_call | solution.py:1098
  338.6 6.0 %convert_bitcast_fusion = f32[256,27,256]{2,0,1:T(8,128)} fusion(bf16[30,256,256]{2,1,0:T(8,128)(2,1)} %get-tuple-element.36), kind=kLoop, calls=%fused_computation | loop fusion | flops 1769472 | bytes 10616832 | tf_op jit(solution)/shard_map/transpose | solution.py:1230
  344.6 0.1 slice_bitcast_fusion
  344.7 1.8 copy.40
  346.5 2.4 reshape.165
  348.9 1.2 broadcast_select_fusion
  350.1 1.8 bitcast_convert_fusion
  351.9 0.7 copy.41
  352.6 0.7 copy.48
  353.3 0.6 copy.49
  353.9 0.6 copy.50
  (45 shorter events, 0.3 us)
Async XLA Ops:
  6.3 3.5 copy-start.9
  7.0 1.4 copy-start.14
  7.0 1.4 copy-start.15
  9.8 3.1 copy-start.12
  9.8 3.9 %copy-start.13 = (bf16[160,256]{1,0:T(8,128)(2,1)S(1)}, bf16[160,256]{1,0:T(8,128)(2,1)}, u32[]{:S(2)}) copy-start(bf16[160,256]{1,0:T(8,128)(2,1)} %param.19) | copy-start | bytes 245764
  137.1 1.5 copy-start.16
  137.1 2.8 copy-start
  137.1 2.8 copy-start.3
  137.1 2.8 copy-start.4
  137.2 2.8 copy-start.5
  137.2 2.8 copy-start.6
  137.2 2.8 copy-start.7
  176.3 0.8 copy-start.1
  177.1 0.8 copy-start.2
  178.0 0.6 copy-start.8
  338.6 6.0 %copy-start.10 = (bf16[8,24,16,256]{3,2,1,0:T(8,128)(2,1)S(1)}, bf16[8,24,16,256]{3,2,1,0:T(8,128)(2,1)}, u32[]{:S(2)}) copy-start(bf16[8,24,16,256]{3,2,1,0:T(8,128)(2,1)} %get-tuple-element.35) | copy-start | bytes 4718596
  348.9 3.7 %copy-start.11 = (f32[160,256]{1,0:T(8,128)S(1)}, f32[160,256]{1,0:T(8,128)}, u32[]{:S(2)}) copy-start(f32[160,256]{1,0:T(8,128)} %get-tuple-element.89) | copy-start | bytes 491524
where the time goes:
time: 359 us; the launch traced here: 355 us
  Pallas kernels  317 us (88%)
  local copies, waits for them, and re-layouts  19.2 us (5%)
  other arithmetic  16.5 us (5%)
    pallas_call x1, Pallas kernels, conv_backward(): pl.pallas_call(functools.partial(back_kernel, pn), out_shape=(shape((TAPS...  158 us
    pallas_call x1, Pallas kernels, conv_forward(): pl.pallas_call(functools.partial(conv_kernel, pn), out_shape=(shape((4, p...  123 us
    pallas_call x1, Pallas kernels, norms(): pl.pallas_call(functools.partial(norm_kernel, pn), out_shape=(shape((4, p...  36.2 us

commit v1 on v0

--- a/solution.py
+++ b/solution.py
@@ -131,6 +131,9 @@
     help_up, help_down = (slab == n - 2) & (col == 1), (slab == 1) & (col == 0)
     half_rows = pn.cs // 2
 
+    def order(k):
+        return k - k // 7 + 3 * (k // 6 - k // 7)
+
     def taps(g):
         return pl.ds(3 * g, 3)
 
@@ -206,7 +209,8 @@
             own_copy(g).start()
             return carry
 
-    lax.fori_loop(0, GROUPS, begin, 0)
+    early = 6
+    lax.fori_loop(0, early, lambda k, carry: begin(order(k), carry), 0)
 
     cot_sent = []
     for cc in range(1, pn.C):
@@ -243,6 +247,15 @@
     def _():
         ring[pl.ds(MARGIN + H, MARGIN)] = jnp.zeros((MARGIN, pn.C * bp, pn.cs), BF16)
 
+    def pass_many(first, end):
+        def one(k, carry):
+            pass_on(order(k))
+            return carry
+
+        if pn.exchange:
+            lax.fori_loop(first, end, one, 0)
+
+    pass_many(0, 3)
     for c in sent:
         c.wait()
     keep.wait()
@@ -262,15 +275,7 @@
     def _():
         margin_up().start()
 
-    def pass_many(first, end):
-        def one(g, carry):
-            pass_on(g)
-            return carry
-
-        if pn.exchange:
-            lax.fori_loop(first, end, one, 0)
-
-    pass_many(0, 3)
+    lax.fori_loop(early, GROUPS, lambda k, carry: begin(order(k), carry), 0)
 
     def assemble(rp, carry):
         pair = ring[pl.ds(2 * rp, 2)].reshape(2 * pn.C * bp, pn.cs)
@@ -281,6 +286,7 @@
         return carry
 
     lax.fori_loop(MARGIN // 2, (MARGIN + H) // 2, assemble, 0, unroll=6)
+    pass_many(3, 5)
     for c in cot_sent:
         c.wait()
     cot_keep.wait()
@@ -291,7 +297,7 @@
     proj_keep.wait()
     for k in range(1, pn.C):
         proj_col(k).start()
-    pass_many(3, 5)
+    pass_many(5, 6)
 
     @pl.when(slab > 0)
     def _():
@@ -338,17 +344,27 @@
         for r in range(many):
             pbuf[slot, (many * rb + r) // 2, r % 2] = y[r * px:(r + 1) * px].astype(BF16)
 
-    def far(g):
-        if g + 5 < GROUPS:
-            pass_many(g + 5, g + 6)
-        w_wait(g)
+    def far(k):
+        if k in (2, 4, 6, 8):
+            pass_many(5 + k // 2, 6 + k // 2)
+        w_wait(order(k))
+
+    def point(rb, carry):
+        at = pl.ds(pl.multiple_of((rb * many + pn.hb) * px, 16), many * px)
+        scatter(0, rb, dot(xs[3, at], wbuf[POINT]))
+        return carry
 
     for branch in (1, 2, 3):
         step = pn.steps[branch - 1]
+        if branch == 3:
+            far(6)
+            lax.fori_loop(0, MEMBERS // many, point, 0)
+            first_stage(0).start()
+            middle(2)
         for i in (-1, 0, 1):
             g = 3 * (branch - 1) + i + 1
             mask_at = (2 * (branch - 1) + (i + 1) // 2) * H
-            far(g)
+            far(g + branch // 3)
 
             def block(rb, carry, step=step, i=i, g=g, mask_at=mask_at, branch=branch):
                 at = pl.multiple_of(rb * many * px, 16)
@@ -371,19 +387,8 @@
 
             lax.fori_loop(0, MEMBERS // many, block, 0)
             if i == 0 and branch > 1:
-                middle(branch - 1)
+                middle(branch - 1 if branch == 2 else 0)
         first_stage(branch).start()
-
-    far(GROUPS - 1)
-
-    def point(rb, carry):
-        at = pl.ds(pl.multiple_of((rb * many + pn.hb) * px, 16), many * px)
-        scatter(0, rb, dot(xs[3, at], wbuf[POINT]))
-        return carry
-
-    lax.fori_loop(0, MEMBERS // many, point, 0)
-    first_stage(0).start()
-    middle(3)
 
     sums = dot(hot_t[...], xs[3, pl.ds(pn.hb * px, pn.own)])
     means = sums * inv_counts[...]
@@ -391,8 +396,8 @@
     p4_out[...] = split_dot(dot, means, wbuf[POOL])
     w_save = pltpu.make_async_copy(wbuf, w_out, o_s.at[1])
     w_save.start()
-    middle(0)
-    for slot in (1, 2, 3):
+    middle(3)
+    for slot in (1, 2, 0):
         last(slot)
     for k in range(1, pn.C):
         proj_col(k).wait()
@@ -407,7 +412,7 @@
             return carry
 
         lax.fori_loop(0, GROUPS, settled, 0)
-    last(0)
+    last(3)
     x_save.wait()
     w_save.wait()
 
@@ -638,18 +643,10 @@
     )(p, p4, gains, biases, valid, pixels, w_proj, cot, hot, hot_t, sel_t)
 
 
-BACK = tuple((b, i) for b in (1, 2, 3) for i in (-1, 1)) + tuple((b, 0) for b in (1, 2, 3))
-
-
-def group_of(k):
-    middle = k // 6
-    return (1 - middle) * (3 * (k // 2) + 2 * (k % 2)) + middle * jnp.minimum(1 + 3 * (k - 6), GROUPS - 1)
-
-
 def back_kernel(pn, q_in, x_in, w_in, dproj_in, q4, means, hot_px, inv_counts, masks, lane_masks, shifts, sel_t,
                 dw_out, dx_out, dproj_out,
                 xs, wbuf, qraw, qs, qt, dxe, dwbuf, inn, hsend, hrecv, pack, dp1, dps, dp2, dpf,
-                l_s, q_s, q_r, k_s, k_r, f_s, f_r, n_s, n_r, e_s, e_r, g_s, g_r, h_s, h_r, x_s, x_r,
+                l_s, q_s, q_r, k_s, k_r, f_s, f_r, n_s, n_r, e_s, e_r, g_s, g_r, b_s, b_r, h_s, h_r, x_s, x_r,
                 p1_s, p1_r, p2_s, p2_r, p3_s, p3_r):
     row, col = lax.axis_index("row"), lax.axis_index("col")
     slab, x = row // pn.G, lax.rem(row, pn.G)
@@ -700,9 +697,9 @@
     slots = (1, 2, 3, 0)
     for slot in slots:
         to_y(slot).start()
-        to_x(slot).start()
         to_partner(slot).start()
         kept(slot).start()
+    to_x(slots[0]).start()
 
     block_rows = 5 * pn.width // MEMBERS
     home_slab = me // pn.G
@@ -722,11 +719,6 @@
     def dproj_give(c):
         return remote(dpf, dproj_out, p3_s.at[c], p3_r.at[0], (slab * pn.G + lax.rem(me, pn.G), c))
 
-    if pn.exchange:
-        for kk in range(1, MEMBERS):
-            dproj_slab(kk).start()
-        dproj_own().start()
-
     def clear(rb, carry):
         dxe[pl.ds(pl.multiple_of(rb * px, 16), px)] = jnp.zeros((px, pn.cs), F32)
         return carry
@@ -737,6 +729,8 @@
         to_y(slot).wait()
         on_to_x(slot).start()
         passed(slot, 0).start()
+        if slot != slots[-1]:
+            to_x(slots[slots.index(slot) + 1]).start()
 
     def receive_x(slot):
         to_x(slot).wait()
@@ -775,21 +769,24 @@
     def relay(g, up):
         side, to = (0, slab + 1) if up else (1, slab - 1)
         return remote(part_of(inn.at[side], g, 1), part_of(inn.at[side], g, 1), e_s.at[g], n_r.at[side, 1, g],
-                      (to * pn.G + x, col + 2))
-
-    def each_link(g, act):
+                      (to * pn.G + x, col))
+
+    def early_links(g, act):
         for going, up, around in ((rising, True, detour_up), (falling, False, detour_down)):
-            @pl.when(going)
-            def _(up=up):
-                act(link(g, 0, up))
-
             @pl.when(going & jnp.logical_not(around))
             def _(up=up):
-                act(link(g, 1, up))
+                for half in (0, 1):
+                    act(link(g, half, up))
 
             @pl.when(around)
             def _(up=up):
                 act(detour(g, up))
+
+    def late_links(g, act):
+        for around, up in ((detour_up, True), (detour_down, False)):
+            @pl.when(around)
+            def _(up=up):
+                act(link(g, 0, up))
 
     def arrived(g, side):
         for half in (0, 1):
@@ -799,166 +796,244 @@
     def add(g, side):
         dwbuf[taps(g)] = (dwbuf[taps(g)].astype(F32) + inn[side, taps(g)].astype(F32)).astype(BF16)
 
-    def share_y(g):
-        return remote(dwbuf.at[taps(g)], dw_out.at[taps(g)], g_s.at[0, g], g_r.at[g], (row, lax.rem(col + 2, pn.C)))
-
-    def share_core(g):
-        return remote(dwbuf.at[taps(g)], dw_out.at[taps(g)], g_s.at[1, g], g_r.at[g], partner)
-
-    def share_on(g):
-        return remote(dw_out.at[taps(g)], dw_out.at[taps(g)], g_s.at[0, g], g_r.at[g], partner)
-
-    shared_on = home_of(pn, lax.rem(col + 2, pn.C)) == slab
-
-    def landed(g):
-        pltpu.make_async_copy(dw_out.at[taps(g)], dw_out.at[taps(g)], g_r.at[g]).wait()
-
-    def serve(k, carry):
-        g = group_of(k)
-        for role, up in ((relay_up, True), (relay_down, False)):
-            @pl.when(role)
+    close_a, close_b = closing & jnp.logical_not(first), ((slab == 1) & (col == 0)) | ((slab == n - 2) & (col == 1))
+    end_closing, end_getting = closing & first, first & (home_of(pn, lax.rem(col + 2, pn.C)) == slab)
+    across = (row, lax.rem(col + 2, pn.C))
+
+    def share_y(g, half, src):
+        return remote(src, part_of(dw_out, g, half), g_s.at[0, half, g], g_r.at[half, g], across)
+
+    def share_core(g, half, src):
+        return remote(src, part_of(dw_out, g, half), g_s.at[1, half, g], g_r.at[half, g], partner)
+
+    def share_on(g, half):
+        return remote(part_of(dw_out, g, half), part_of(dw_out, g, half), g_s.at[0, half, g], g_r.at[half, g], partner)
+
+    def share(g, half, src):
+        share_y(g, half, src).start()
+        share_core(g, half, src).start()
+        pltpu.make_async_copy(src, part_of(dw_out, g, half), g_r.at[half, g]).start()
+
+    def landed(g, half):
+        at = part_of(dw_out, g, half)
+        pltpu.make_async_copy(at, at, g_r.at[half, g]).wait()
+
+    def partial(g, side):
+        return remote(part_of(dwbuf, g, 1), part_of(inn.at[1 - side], g, 0), b_s.at[g], b_r.at[g], (row, col - 2))
+
+    rows_of = (pl.ds(0, half_rows), pl.ds(half_rows, half_rows))
+
+    def from_far(g):
+        for here, side in ((slab == 1, 1), (slab == n - 2, 0)):
+            @pl.when(close_a & here)
+            def _(side=side):
+                arrived(g, side)
+                add(g, side)
+                partial(g, side).start()
+
+    def close_half(g):
+        for here, side in ((slab == 1, 0), (slab == n - 2, 1)):
+            @pl.when(close_a & here)
+            def _(side=side):
+                at = part_of(inn.at[side], g, 0)
+                pltpu.make_async_copy(at, at, n_r.at[side, 0, g]).wait()
+                dwbuf[taps(g), rows_of[0]] = (
+                    dwbuf[taps(g), rows_of[0]].astype(F32) + inn[side, taps(g), rows_of[0]].astype(F32)
+                ).astype(BF16)
+                share(g, 0, part_of(dwbuf, g, 0))
+
+            @pl.when(close_b & here)
+            def _(side=side):
+                at = part_of(inn.at[side], g, 1)
+                pltpu.make_async_copy(at, at, n_r.at[side, 1, g]).wait()
+                at = part_of(inn.at[side], g, 0)
+                pltpu.make_async_copy(at, at, b_r.at[g]).wait()
+                inn[side, taps(g), rows_of[1]] = (
+                    inn[side, taps(g), rows_of[1]].astype(F32) + inn[side, taps(g), rows_of[0]].astype(F32)
+                ).astype(BF16)
+                share(g, 1, part_of(inn.at[side], g, 1))
+
+    def relay_many(start, end):
+        def one(g, carry):
+            for role, up in ((relay_up, True), (relay_down, False)):
+                @pl.when(role)
+                def _(up=up):
+                    at = part_of(inn.at[0 if up else 1], g, 1)
+                    pltpu.make_async_copy(at, at, e_r.at[g]).wait()
+                    relay(g, up).start()
+            return carry
+
+        if pn.exchange:
+            lax.fori_loop(start, end, one, 0)
+
+    def late(start, end):
+        def one(g, carry):
+            late_links(g, lambda c: c.start())
+            return carry
+
+        if pn.exchange:
+            lax.fori_loop(start, end, one, 0)
+        relay_many(start, end)
+
+    def pass_on(g):
+        for going, up in ((rising, True), (falling, False)):
+            @pl.when(going & jnp.logical_not(first))
             def _(up=up):
-                side = 0 if up else 1
-                at = part_of(inn.at[side], g, 1)
-                pltpu.make_async_copy(at, at, e_r.at[g]).wait()
-                relay(g, up).start()
-
-        @pl.when(rising & jnp.logical_not(first))
+                arrived(g, 0 if up else 1)
+                add(g, 0 if up else 1)
+                for half in (0, 1):
+                    link(g, half, up).start()
+
+    def close(g):
+        for here, side in ((slab == 0, 1), (slab == n - 1, 0)):
+            @pl.when(end_closing & here)
+            def _(side=side):
+                arrived(g, side)
+                add(g, side)
+                for half in (0, 1):
+                    share(g, half, part_of(dwbuf, g, half))
+
+    def serve(g):
+        if not pn.exchange:
+            return
+        if g < GROUPS:
+            pass_on(g)
+        if g > 1:
+            close(g - 2)
+            from_far(g - 2)
+
+    def last_round(g, carry):
+        @pl.when(g < GROUPS)
         def _():
-            arrived(g, 0)
-            add(g, 0)
-            for half in (0, 1):
-                link(g, half, True).start()
-
-        @pl.when(falling & jnp.logical_not(first))
+            close_half(g)
+
+        @pl.when(g > 1)
         def _():
-            arrived(g, 1)
-            add(g, 1)
-            for half in (0, 1):
-                link(g, half, False).start()
-
-        @pl.when(closing)
+            before = jnp.maximum(g - 2, 0)
+            for half, role in ((0, end_getting | close_b), (1, end_getting | close_a)):
+                @pl.when(role)
+                def _(half=half):
+                    landed(before, half)
+                    share_on(before, half).start()
+
+        return carry
+
+    def start_group(g):
+        if not pn.exchange:
+            return
+
+        @pl.when(first)
         def _():
-            @pl.when(slab > 0)
-            def _():
-                arrived(g, 0)
-                add(g, 0)
-
-            @pl.when(slab < n - 1)
-            def _():
-                arrived(g, 1)
-                add(g, 1)
-
-            share_y(g).start()
-            share_core(g).start()
-            pltpu.make_async_copy(dwbuf.at[taps(g)], dw_out.at[taps(g)], g_r.at[g]).start()
-
-        @pl.when(shared_on & (k > 1))
-        def _():
-            before = group_of(jnp.maximum(k - 2, 0))
-            landed(before)
-            share_on(before).start()
-
-        return carry
+            early_links(g, lambda c: c.start())
+
+    def weight_gradients(branch):
+        qt[...] = qraw[branch].T
+        for i in (-1, 0, 1):
+            g = 3 * (branch - 1) + i + 1
+            q_turned = qt[...]
+            if i != 0:
+                q_turned = q_turned * lane_masks[pl.ds(2 * (branch - 1) + (i + 1) // 2, 1)]
+            window = pl.ds((pn.hb + i * pn.steps[branch - 1]) * px, pn.own)
+            for j in (-1, 0, 1):
+                dwbuf[3 * g + j + 1] = dot(q_turned, xs[3 + j * branch, window]).T.astype(BF16)
+            if branch < 3:
+                start_group(g)
+
+    def feature_gradients(branch):
+        def turn(rp, carry):
+            at = pl.multiple_of(rp * 2 * S, 16)
+            moved = dot(shifts[pl.ds((branch - 1) * 4 * S, 4 * S)], qraw[branch, pl.ds(at, 2 * S)]).astype(BF16)
+            qs[branch - 1, 0, pl.ds(at, 2 * S)] = moved[:2 * S]
+            qs[branch - 1, 1, pl.ds(at, 2 * S)] = moved[2 * S:]
+            return carry
+
+        lax.fori_loop(0, H // 2, turn, 0, unroll=6)
+        for i in (-1, 0, 1):
+            g = 3 * (branch - 1) + i + 1
+            mask_at = (2 * (branch - 1) + (i + 1) // 2) * H
+
+            def block(rb, carry, i=i, g=g, mask_at=mask_at):
+                at = pl.ds(pl.multiple_of(rb * many * px, 16), many * px)
+                y = dot_nt(qs[branch - 1, 0, at], wbuf[3 * g])
+                y = y + dot_nt(qraw[branch, at], wbuf[3 * g + 1])
+                y = y + dot_nt(qs[branch - 1, 1, at], wbuf[3 * g + 2])
+                if i != 0:
+                    y = jnp.concatenate(
+                        [y[r * S:(r + 1) * S] * masks[mask_at + rb * many * pn.rpb + r] for r in range(many * pn.rpb)], axis=0
+                    )
+                to = pl.ds(pl.multiple_of((rb * many + pn.hb + i * pn.steps[branch - 1]) * px, 16), many * px)
+                dxe[to] = dxe[to] + y
+                return carry
+
+            lax.fori_loop(0, MEMBERS // many, block, 0)
 
     receive_y(1)
     receive_y(2)
     load_x.wait()
     load_w.wait()
     receive_x(1)
+    received(1)
+    weight_gradients(1)
     receive_y(3)
-
-    def start_group(k):
-        if not pn.exchange:
-            return
-        g = group_index(k)
-
-        @pl.when(first)
+    receive_x(2)
+    feature_gradients(1)
+    receive_y(0)
+    received(2)
+    weight_gradients(2)
+    receive_x(3)
+    serve(0)
+    feature_gradients(2)
+    received(3)
+    receive_x(0)
+    if pn.exchange:
+        for kk in range(1, MEMBERS):
+            dproj_slab(kk).start()
+        dproj_own().start()
+    serve(1)
+    weight_gradients(3)
+    serve(2)
+    feature_gradients(3)
+
+    hsend[0] = dxe[pl.ds(0, pn.hb * px)].astype(BF16)
+    hsend[1] = dxe[pl.ds((pn.hb + MEMBERS) * px, pn.hb * px)].astype(BF16)
+
+    @pl.when(slab > 0)
+    def _():
+        remote(hsend.at[0], hrecv.at[1], h_s.at[0], h_r.at[1], member(slab - 1, me)).start()
+
+    @pl.when(slab < n - 1)
+    def _():
+        remote(hsend.at[1], hrecv.at[0], h_s.at[1], h_r.at[0], member(slab + 1, me)).start()
+
+    for g in (6, 7, 8):
+        start_group(g)
+    late(0, GROUPS - 1)
+    serve(3)
+
+    if pn.exchange:
+        for kk in range(1, MEMBERS):
+            dproj_slab(kk).wait()
+        dproj_own().wait()
+        total = dp1[0].astype(F32)
+        for m in range(1, MEMBERS):
+            total = total + dp1[m].astype(F32)
+        dps[...] = total.astype(BF16)
+
+        @pl.when(slab != home_slab)
         def _():
-            each_link(g, lambda c: c.start())
-
-    def group_index(k):
-        if k < len(BACK):
-            b, i = BACK[k]
-            return 3 * (b - 1) + i + 1
-        return GROUPS - 1
-
-    for k, (branch, i) in enumerate(BACK):
-        step = pn.steps[branch - 1]
-        g = group_index(k)
-        if i == -1:
-            received(branch)
-            if branch == 2:
-                receive_y(0)
-            receive_x(branch + 1 if branch < 3 else 0)
-
-            def turn(rp, carry, branch=branch):
-                at = pl.multiple_of(rp * 2 * S, 16)
-                moved = dot(shifts[pl.ds((branch - 1) * 4 * S, 4 * S)], qraw[branch, pl.ds(at, 2 * S)]).astype(BF16)
-                qs[branch - 1, 0, pl.ds(at, 2 * S)] = moved[:2 * S]
-                qs[branch - 1, 1, pl.ds(at, 2 * S)] = moved[2 * S:]
-                return carry
-
-            lax.fori_loop(0, H // 2, turn, 0, unroll=6)
-        if i != 1:
-            qt[...] = qraw[branch].T
-        q_turned = qt[...]
-        if i != 0:
-            q_turned = q_turned * lane_masks[pl.ds(2 * (branch - 1) + (i + 1) // 2, 1)]
-        window = pl.ds((pn.hb + i * step) * px, pn.own)
-        for j in (-1, 0, 1):
-            dwbuf[3 * g + j + 1] = dot(q_turned, xs[3 + j * branch, window]).T.astype(BF16)
-        start_group(k)
-        mask_at = (2 * (branch - 1) + (i + 1) // 2) * H
-
-        def block(rb, carry, branch=branch, i=i, step=step, g=g, mask_at=mask_at):
-            at = pl.ds(pl.multiple_of(rb * many * px, 16), many * px)
-            y = dot_nt(qs[branch - 1, 0, at], wbuf[3 * g])
-            y = y + dot_nt(qraw[branch, at], wbuf[3 * g + 1])
-            y = y + dot_nt(qs[branch - 1, 1, at], wbuf[3 * g + 2])
-            if i != 0:
-                y = jnp.concatenate(
-                    [y[r * S:(r + 1) * S] * masks[mask_at + rb * many * pn.rpb + r] for r in range(many * pn.rpb)], axis=0
-                )
-            to = pl.ds(pl.multiple_of((rb * many + pn.hb + i * step) * px, 16), many * px)
-            dxe[to] = dxe[to] + y
-            return carry
-
-        lax.fori_loop(0, MEMBERS // many, block, 0)
-        if k == 5:
-            hsend[0] = dxe[pl.ds(0, pn.hb * px)].astype(BF16)
-            hsend[1] = dxe[pl.ds((pn.hb + MEMBERS) * px, pn.hb * px)].astype(BF16)
-
-            @pl.when(slab > 0)
-            def _():
-                remote(hsend.at[0], hrecv.at[1], h_s.at[0], h_r.at[1], member(slab - 1, me)).start()
-
-            @pl.when(slab < n - 1)
-            def _():
-                remote(hsend.at[1], hrecv.at[0], h_s.at[1], h_r.at[0], member(slab + 1, me)).start()
-
-        if pn.exchange and k == 3:
-            for kk in range(1, MEMBERS):
-                dproj_slab(kk).wait()
-            dproj_own().wait()
-            total = dp1[0].astype(F32)
-            for m in range(1, MEMBERS):
-                total = total + dp1[m].astype(F32)
-            dps[...] = total.astype(BF16)
-
-            @pl.when(slab != home_slab)
-            def _():
-                dproj_home().start()
-
-            @pl.when(slab == home_slab)
-            def _():
-                pltpu.make_async_copy(dps, dp2.at[slab], p2_r.at[slab]).start()
+            dproj_home().start()
+
+        @pl.when(slab == home_slab)
+        def _():
+            pltpu.make_async_copy(dps, dp2.at[slab], p2_r.at[slab]).start()
 
     received(0)
     dwbuf[POOL] = dot_tn(means[...].astype(BF16), q4[...]).astype(BF16)
     dwbuf[POINT] = dot(qraw[0].T, xs[3, pl.ds(pn.hb * px, pn.own)]).T.astype(BF16)
     dwbuf[TAPS - 1] = jnp.zeros((pn.cs, pn.width), BF16)
     start_group(GROUPS - 1)
+    late(GROUPS - 1, GROUPS)
+    serve(4)
     pooled = dot_nt(q4[...], wbuf[POOL]) * inv_counts[...]
     pooled_high = pooled.astype(BF16)
     pooled_low = (pooled - pooled_high.astype(F32)).astype(BF16)
@@ -972,8 +1047,56 @@
         return carry
 
     lax.fori_loop(0, MEMBERS // many, finish, 0)
+    serve(5)
+
+    @pl.when(slab > 0)
+    def _():
+        remote(hsend.at[0], hrecv.at[1], h_s.at[0], h_r.at[1], member(slab - 1, me)).wait_send()
+        remote(hsend.at[1], hrecv.at[0], h_s.at[1], h_r.at[0], member(slab - 1, me)).wait_recv()
+
+    @pl.when(slab < n - 1)
+    def _():
+        remote(hsend.at[1], hrecv.at[0], h_s.at[1], h_r.at[0], member(slab + 1, me)).wait_send()
+        remote(hsend.at[0], hrecv.at[1], h_s.at[0], h_r.at[1], member(slab + 1, me)).wait_recv()
+
+    @pl.when(slab == 0)
+    def _():
+        hrecv[0] = jnp.zeros((pn.hb * px, pn.cs), BF16)
+
+    @pl.when(slab == n - 1)
+    def _():
+        hrecv[1] = jnp.zeros((pn.hb * px, pn.cs), BF16)
+
+    for rb in range(pn.hb):
+        low, high = (pn.hb + rb) * px, (MEMBERS + rb) * px
+        dxe[pl.ds(low, px)] = dxe[pl.ds(low, px)] + hrecv[0, pl.ds(rb * px, px)].astype(F32)
+        dxe[pl.ds(high, px)] = dxe[pl.ds(high, px)] + hrecv[1, pl.ds(rb * px, px)].astype(F32)
+
+    def packing(rp, carry):
+        pair = dxe[pl.ds(pl.multiple_of(pn.hb * px + rp * 2 * S, 16), 2 * S)].astype(BF16)
+        pack[pl.ds(2 * rp, 2)] = dot(sel_t[...], pair).astype(BF16).reshape(2, pn.C * bp, pn.cs)
+        return carry
+
+    lax.fori_loop(0, H // 2, packing, 0, unroll=6)
+    back = []
+    for kk in range(1, MEMBERS):
+        other = lax.rem(me + kk, MEMBERS)
+        xo, co = other // pn.C, lax.rem(other, pn.C)
+        c = remote(pack.at[pl.ds(xo * h, h), pl.ds(pl.multiple_of(co * bp, bp), bp)], dx_out.at[slice_of(pn, me)], x_s.at[kk], x_r.at[kk],
+                   member(slab, other))
+        c.start()
+        back.append(c)
+    c = pltpu.make_async_copy(pack.at[pl.ds(x * h, h), pl.ds(pl.multiple_of(col * bp, bp), bp)], dx_out.at[slice_of(pn, me)], x_r.at[0])
+    c.start()
+    back.append(c)
+
     if pn.exchange:
-        lax.fori_loop(0, 6, serve, 0)
+        done = 0
+        for g, end in ((6, 1), (7, 3), (8, 4), (9, 6), (10, 7), (11, 8), (None, GROUPS + 2)):
+            if g is not None:
+                serve(g)
+            lax.fori_loop(done, end, last_round, 0)
+            done = end
 
         @pl.when(slab == home_slab)
         def _():
@@ -992,75 +1115,32 @@
                 def _(c=c):
                     dproj_give(c).start()
 
-    @pl.when(slab > 0)
-    def _():
-        remote(hsend.at[0], hrecv.at[1], h_s.at[0], h_r.at[1], member(slab - 1, me)).wait_send()
-        remote(hsend.at[1], hrecv.at[0], h_s.at[1], h_r.at[0], member(slab - 1, me)).wait_recv()
-
-    @pl.when(slab < n - 1)
-    def _():
-        remote(hsend.at[1], hrecv.at[0], h_s.at[1], h_r.at[0], member(slab + 1, me)).wait_send()
-        remote(hsend.at[0], hrecv.at[1], h_s.at[0], h_r.at[1], member(slab + 1, me)).wait_recv()
-
-    @pl.when(slab == 0)
-    def _():
-        hrecv[0] = jnp.zeros((pn.hb * px, pn.cs), BF16)
-
-    @pl.when(slab == n - 1)
-    def _():
-        hrecv[1] = jnp.zeros((pn.hb * px, pn.cs), BF16)
-
-    for rb in range(pn.hb):
-        low, high = (pn.hb + rb) * px, (MEMBERS + rb) * px
-        dxe[pl.ds(low, px)] = dxe[pl.ds(low, px)] + hrecv[0, pl.ds(rb * px, px)].astype(F32)
-        dxe[pl.ds(high, px)] = dxe[pl.ds(high, px)] + hrecv[1, pl.ds(rb * px, px)].astype(F32)
-
-    def packing(rp, carry):
-        pair = dxe[pl.ds(pl.multiple_of(pn.hb * px + rp * 2 * S, 16), 2 * S)].astype(BF16)
-        pack[pl.ds(2 * rp, 2)] = dot(sel_t[...], pair).astype(BF16).reshape(2, pn.C * bp, pn.cs)
-        return carry
-
-    lax.fori_loop(0, H // 2, packing, 0, unroll=6)
-    back = []
-    for kk in range(1, MEMBERS):
-        other = lax.rem(me + kk, MEMBERS)
-        xo, co = other // pn.C, lax.rem(other, pn.C)
-        c = remote(pack.at[pl.ds(xo * h, h), pl.ds(pl.multiple_of(co * bp, bp), bp)], dx_out.at[slice_of(pn, me)], x_s.at[kk], x_r.at[kk],
-                   member(slab, other))
-        c.start()
-        back.append(c)
-    c = pltpu.make_async_copy(pack.at[pl.ds(x * h, h), pl.ds(pl.multiple_of(col * bp, bp), bp)], dx_out.at[slice_of(pn, me)], x_r.at[0])
-    c.start()
-    back.append(c)
-
-    if pn.exchange:
-        lax.fori_loop(6, GROUPS, serve, 0)
-
-        @pl.when(shared_on)
-        def _():
-            for k in (GROUPS - 2, GROUPS - 1):
-                landed(group_index(k))
-                share_on(group_index(k)).start()
-
         def settle(g, carry):
-            each_link(g, lambda c: c.wait_send())
+            early_links(g, lambda c: c.wait_send())
+            late_links(g, lambda c: c.wait_send())
             for role, up in ((relay_up, True), (relay_down, False)):
                 @pl.when(role)
                 def _(up=up):
                     relay(g, up).wait_send()
 
-            @pl.when(closing)
+            @pl.when(close_a)
             def _():
-                share_y(g).wait_send()
-                share_core(g).wait_send()
-
-            @pl.when(shared_on)
-            def _():
-                share_on(g).wait_send()
-
-            @pl.when(jnp.logical_not(shared_on))
-            def _():
-                landed(g)
+                partial(g, 0).wait_send()
+
+            for half, gives, passes in ((0, end_closing | close_a, end_getting | close_b),
+                                        (1, end_closing | close_b, end_getting | close_a)):
+                @pl.when(gives)
+                def _(half=half):
+                    share_y(g, half, part_of(dwbuf, g, half)).wait_send()
+                    share_core(g, half, part_of(dwbuf, g, half)).wait_send()
+
+                @pl.when(passes)
+                def _(half=half):
+                    share_on(g, half).wait_send()
+
+                @pl.when(jnp.logical_not(passes))
+                def _(half=half):
+                    landed(g, half)
 
             return carry
 
@@ -1079,7 +1159,7 @@
 
         pltpu.make_async_copy(dproj_out, dproj_out, p3_r.at[0]).wait()
     else:
-        c = pltpu.make_async_copy(dwbuf, dw_out, g_r.at[0])
+        c = pltpu.make_async_copy(dwbuf, dw_out, g_r.at[0, 0])
         c.start()
         c.wait()
         dproj_out[...] = jnp.zeros(dproj_out.shape, F32)
@@ -1121,7 +1201,8 @@
             pltpu.VMEM((n, block_rows, pn.width), BF16),
             pltpu.VMEM((block_rows, pn.width), F32),
             dma((6,)), dma((4, 3)), dma((4, 3)), dma((4,)), dma((4,)), dma((4, 3)), dma((4, 3)),
-            dma((2, GROUPS)), dma((2, 2, GROUPS)), dma((GROUPS,)), dma((GROUPS,)), dma((2, GROUPS)), dma((GROUPS,)),
+            dma((2, GROUPS)), dma((2, 2, GROUPS)), dma((GROUPS,)), dma((GROUPS,)), dma((2, 2, GROUPS)), dma((2, GROUPS)),
+            dma((GROUPS,)), dma((GROUPS,)),
             dma((2,)), dma((2,)), dma((MEMBERS,)), dma((MEMBERS,)),
             dma((MEMBERS,)), dma((MEMBERS,)), dma((1,)), dma((n,)), dma((pn.C,)), dma((1,)),
         ],

time: 359 us -> 313 us (0.87)
  Pallas kernels: 317 us -> 272 us
    pallas_call x1, Pallas kernels: 158 us -> 133 us  [conv_backward(): pl.pallas_call(functools.partial(back_kernel, pn), out_shape=(shape((TAPS...]
    pallas_call x1, Pallas kernels: 123 us -> 101 us  [conv_forward(): pl.pallas_call(functools.partial(conv_kernel, pn), out_shape=(shape((4, p...]
where the time goes in v1:
time: 313 us; the launch traced here: 310 us
  Pallas kernels  272 us (87%)
  local copies, waits for them, and re-layouts  19.2 us (6%)
  other arithmetic  16.5 us (5%)
    pallas_call x1, Pallas kernels, conv_backward(): pl.pallas_call(functools.partial(back_kernel, pn), out_shape=(shape((TAPS...  133 us
    pallas_call x1, Pallas kernels, conv_forward(): pl.pallas_call(functools.partial(conv_kernel, pn), out_shape=(shape((4, p...  101 us
    pallas_call x1, Pallas kernels, norms(): pl.pallas_call(functools.partial(norm_kernel, pn), out_shape=(shape((4, p...  38.4 us

profile of v1, /device:TPU:9, one launch (start us, length us, event | category | flops | bytes accessed | tf_op | source)
XLA Modules:
  0.0 309.7 jit_solution(8437494592940815602)
XLA Ops:
  0.7 0.8 reduce-window.8
  1.5 0.1 convert_reduce_fusion
  1.6 0.1 compare_bitcast_fusion
  1.7 0.7 reshape.166.masks
  2.5 0.2 broadcast_in_dim.109
  2.6 0.9 reshape.159.hot_t
  3.5 0.1 convert_reduce_fusion.1
  3.6 0.7 select_reduce_fusion.1
  4.3 0.1 broadcast_compare_fusion
  4.4 1.5 broadcast_select_fusion.1
  5.9 0.4 copy.42
  6.3 0.8 copy.44
  7.1 1.4 pad.21.feats
  8.4 0.6 convert_reduce_fusion.2
  9.0 0.7 copy.36.inv_counts
  9.7 0.1 pad.29.clone
  9.8 3.1 %maximum_maximum_fusion.w_in = bf16[30,256,256]{2,1,0:T(8,128)(2,1)} fusion(bf16[1,256,256]{2,1,0:T(8,128)(2,1)} %bitcast.59, bf16[1,256,256]{2,1,0:T(8,128)(2,1)} %bitcast.60, bf16[27,256,256]{2,1,0:T(8,128)(2,1)S(1)} %bitcast.57, bf16[30]{0:T(256)(128)(2,1)S(1)} %pad.29.clone), kind=kLoop, calls=%fused_computation.1 | loop fusion | flops 5898240 | bytes 7733308 | tf_op jit(solution)/shard_map/concatenate | solution.py:1283
  13.0 0.7 pad.22.cot
  13.7 0.6 pad.23.proj
  14.3 100.8 %conv_forward.1 = (f32[4,336,256]{2,1,0:T(8,128)}, bf16[7,4704,256]{2,1,0:T(8,128)(2,1)}, bf16[30,256,256]{2,1,0:T(8,128)(2,1)}, f32[16,256]{1,0:T(8,128)}, f32[...) custom-call(bf16[8,24,16,256]{3,2,1,0:T(8,128)(2,1)} %pad.21.feats, ...), custom_call_target="tpu_custom_call" | custom-call | tf_op jit(solution)/shard_map/conv_forward/pallas_call | solution.py:426
  115.2 1.2 slice_bitcast_fusion.1
  116.6 0.1 dynamic_slice.3
  116.6 0.2 select_reduce_fusion
  116.8 0.1 fusion.3
  116.9 0.1 reshape.170.valid
  117.0 0.1 fusion.4
  117.1 0.1 broadcast_in_dim.115
  117.2 0.1 reshape.162.hot_t
  118.1 38.4 %norms.1 = (bf16[4,336,256]{2,1,0:T(8,128)(2,1)S(1)}, bf16[16,256]{1,0:T(8,128)(2,1)S(1)}, bf16[1280,256]{1,0:T(8,128)(2,1)S(1)}, bf16[24,16,256]{2,1,0:T(8,128)...) custom-call(f32[4,336,256]{2,1,0:T(8,128)S(1)} %copy-done, f32[16,256]{1,0:T(8,128)S(1)} %copy-done.5, ...), custom_call_target="tpu_custom_call" | custom-call | tf_op jit(solution)/shard_map/norms/pallas_call | solution.py:619
  156.5 0.8 copy-done.1
  157.4 0.8 copy-done.2
  158.2 0.6 copy-done.8
  158.8 0.1 broadcast_in_dim.117
  158.9 0.2 reshape.164
  159.1 0.6 pad.25.lane_masks
  159.7 0.1 fusion
  159.8 0.9 broadcast_in_dim.116
  160.7 132.7 %conv_backward.1 = (bf16[30,256,256]{2,1,0:T(8,128)(2,1)}, bf16[8,24,16,256]{3,2,1,0:T(8,128)(2,1)}, f32[160,256]{1,0:T(8,128)}) custom-call(bf16[4,336,256]{2,1,0:T(8,128)(2,1)} %copy-done.1, bf16[7,4704,256]{2,1,0:T(8,128)(2,1)} %get-tuple-element.30.x_in, bf16[30,256,256]{2,1,0:T(8,128)(2,1)} %get-tuple-element.31.w_in, bf16[1280,256]{1,0:T(8,128)(2,1)} %copy-done.2, ...), custom_call_target="tpu_custom_call" | custom-call | tf_op jit(solution)/shard_map/conv_backward/pallas_call | solution.py:1178
  293.4 6.0 %convert_bitcast_fusion = f32[256,27,256]{2,0,1:T(8,128)} fusion(bf16[30,256,256]{2,1,0:T(8,128)(2,1)} %get-tuple-element.36), kind=kLoop, calls=%fused_computation | loop fusion | flops 1769472 | bytes 10616832 | tf_op jit(solution)/shard_map/transpose | solution.py:1311
  299.4 0.1 slice_bitcast_fusion
  299.5 1.8 copy.40
  301.3 2.4 reshape.165
  303.7 1.2 broadcast_select_fusion
  304.9 1.8 bitcast_convert_fusion
  306.7 0.7 copy.41
  307.4 0.7 copy.48
  308.0 0.6 copy.49
  308.6 0.6 copy.50
  (45 shorter events, 0.3 us)
Async XLA Ops:
  6.3 3.5 %copy-start.9 = (bf16[256,27,256]{2,0,1:T(8,128)(2,1)S(1)}, bf16[256,27,256]{2,0,1:T(8,128)(2,1)}, u32[]{:S(2)}) copy-start(bf16[256,27,256]{2,0,1:T(8,128)(2,1)} %param.17) | copy-start | bytes 10616836
  7.0 1.4 copy-start.14
  7.0 1.4 copy-start.15
  9.8 3.1 %copy-start.12 = (bf16[24,13,256]{2,0,1:T(8,128)(2,1)S(1)}, bf16[24,13,256]{2,0,1:T(8,128)(2,1)}, u32[]{:S(2)}) copy-start(bf16[24,13,256]{2,0,1:T(8,128)(2,1)} %param.22) | copy-start | bytes 479236
  9.8 3.9 %copy-start.13 = (bf16[160,256]{1,0:T(8,128)(2,1)S(1)}, bf16[160,256]{1,0:T(8,128)(2,1)}, u32[]{:S(2)}) copy-start(bf16[160,256]{1,0:T(8,128)(2,1)} %param.19) | copy-start | bytes 245764
  115.2 1.5 copy-start.16
  115.2 2.8 copy-start
  115.2 2.8 copy-start.3
  115.2 2.8 copy-start.4
  115.2 2.8 copy-start.5
  115.2 2.8 copy-start.6
  115.2 2.8 copy-start.7
  156.5 0.8 copy-start.1
  157.4 0.8 copy-start.2
  158.2 0.6 copy-start.8
  293.4 6.0 %copy-start.10 = (bf16[8,24,16,256]{3,2,1,0:T(8,128)(2,1)S(1)}, bf16[8,24,16,256]{3,2,1,0:T(8,128)(2,1)}, u32[]{:S(2)}) copy-start(bf16[8,24,16,256]{3,2,1,0:T(8,128)(2,1)} %get-tuple-element.35) | copy-start | bytes 4718596
  303.6 3.7 %copy-start.11 = (f32[160,256]{1,0:T(8,128)S(1)}, f32[160,256]{1,0:T(8,128)}, u32[]{:S(2)}) copy-start(f32[160,256]{1,0:T(8,128)} %get-tuple-element.89) | copy-start | bytes 491524

commit v2 on v1

--- a/solution.py
+++ b/solution.py
@@ -12,7 +12,7 @@
 MARGIN = 18
 DILATIONS = (6, 12, 18)
 MEMBERS = 8
-TAPS = 30
+TAPS = 29
 POINT, POOL, GROUPS = 27, 28, 10
 MESH = pl.DeviceIdType.MESH
 F32 = jnp.float32
@@ -98,7 +98,7 @@
     return dot_fn(high, b) + dot_fn(low, b)
 
 
-def conv_kernel(pn, feats, w_in, cot, proj, masks, sel, hot_t, inv_counts,
+def conv_kernel(pn, feats, w_in, w_two, cot, proj, masks, sel, hot_t, inv_counts,
                 p_out, x_out, w_out, m_out, p4_out, cot_out, proj_out,
                 ring, xs, wbuf, acc, pbuf, cbuf, sbuf, rbuf, cx,
                 f_s, f_r, h_s, h_r, c_s, c_r, j_s, j_r, t_s, t_r, w_s, w_r, w_l, e_s,
@@ -131,26 +131,33 @@
     help_up, help_down = (slab == n - 2) & (col == 1), (slab == 1) & (col == 0)
     half_rows = pn.cs // 2
 
-    def order(k):
-        return k - k // 7 + 3 * (k // 6 - k // 7)
+    order = (0, 1, 2, 3, 4, 5, 9, 6, 7, 8)
 
     def taps(g):
-        return pl.ds(3 * g, 3)
+        return pl.ds(POINT, 2) if isinstance(g, int) and g == GROUPS - 1 else pl.ds(3 * g, 3)
+
+    def given(g, rows):
+        if isinstance(g, int) and g == GROUPS - 1:
+            return w_two.at[:, rows]
+        return w_in.at[taps(g), rows]
+
+    def half_of(half):
+        return pl.ds(half * half_rows, half_rows)
 
     def part_of(ref, g, half):
-        return ref.at[taps(g), pl.ds(half * half_rows, half_rows)]
-
-    def ship(g, half, up, src):
+        return ref.at[taps(g), half_of(half)]
+
+    def ship(g, half, up, own):
         to = slab + 1 if up else slab - 1
-        return remote(part_of(src, g, half), part_of(wbuf, g, half), w_s.at[int(up), half, g], w_r.at[half, g],
+        return remote(given(g, half_of(half)) if own else part_of(wbuf, g, half), part_of(wbuf, g, half), w_s.at[int(up), half, g], w_r.at[half, g],
                       (to * pn.G + x, col))
 
     def assist(g, up):
         to = slab + 1 if up else slab - 1
-        return remote(part_of(w_in, g, 1), part_of(wbuf, g, 1), e_s.at[g], w_r.at[1, g], (to * pn.G + x, col + 2))
+        return remote(given(g, half_of(1)), part_of(wbuf, g, 1), e_s.at[g], w_r.at[1, g], (to * pn.G + x, col + 2))
 
     def own_copy(g):
-        return pltpu.make_async_copy(w_in.at[taps(g)], wbuf.at[taps(g)], w_l.at[g])
+        return pltpu.make_async_copy(given(g, pl.ds(0, pn.cs)), wbuf.at[taps(g)], w_l.at[g])
 
     def arrived(g):
         for half in (0, 1):
@@ -163,7 +170,7 @@
             def _(up=up):
                 arrived(g)
                 for half in (0, 1):
-                    ship(g, half, up, wbuf).start()
+                    ship(g, half, up, False).start()
 
     def w_wait(g):
         if pn.exchange:
@@ -181,11 +188,11 @@
         for half in (0, 1):
             @pl.when(source & ((slab < n - 2) if half else (slab < n - 1)))
             def _(half=half):
-                act(ship(g, half, True, w_in))
+                act(ship(g, half, True, True))
 
             @pl.when(source & ((slab > 1) if half else (slab > 0)))
             def _(half=half):
-                act(ship(g, half, False, w_in))
+                act(ship(g, half, False, True))
 
         @pl.when(help_up)
         def _():
@@ -210,7 +217,7 @@
             return carry
 
     early = 6
-    lax.fori_loop(0, early, lambda k, carry: begin(order(k), carry), 0)
+    lax.fori_loop(0, early, begin, 0)
 
     cot_sent = []
     for cc in range(1, pn.C):
@@ -248,12 +255,9 @@
         ring[pl.ds(MARGIN + H, MARGIN)] = jnp.zeros((MARGIN, pn.C * bp, pn.cs), BF16)
 
     def pass_many(first, end):
-        def one(k, carry):
-            pass_on(order(k))
-            return carry
-
         if pn.exchange:
-            lax.fori_loop(first, end, one, 0)
+            for k in range(first, end):
+                pass_on(order[k])
 
     pass_many(0, 3)
     for c in sent:
@@ -275,7 +279,8 @@
     def _():
         margin_up().start()
 
-    lax.fori_loop(early, GROUPS, lambda k, carry: begin(order(k), carry), 0)
+    begin(GROUPS - 1, 0)
+    lax.fori_loop(early, GROUPS - 1, begin, 0)
 
     def assemble(rp, carry):
         pair = ring[pl.ds(2 * rp, 2)].reshape(2 * pn.C * bp, pn.cs)
@@ -347,7 +352,7 @@
     def far(k):
         if k in (2, 4, 6, 8):
             pass_many(5 + k // 2, 6 + k // 2)
-        w_wait(order(k))
+        w_wait(order[k])
 
     def point(rb, carry):
         at = pl.ds(pl.multiple_of((rb * many + pn.hb) * px, 16), many * px)
@@ -408,16 +413,17 @@
                 @pl.when(role)
                 def _(up=up):
                     for half in (0, 1):
-                        ship(g, half, up, wbuf).wait_send()
+                        ship(g, half, up, False).wait_send()
             return carry
 
-        lax.fori_loop(0, GROUPS, settled, 0)
+        lax.fori_loop(0, GROUPS - 1, settled, 0)
+        settled(GROUPS - 1, 0)
     last(3)
     x_save.wait()
     w_save.wait()
 
 
-def conv_forward(pn, feats, w, cot, proj, masks, sel, hot_t, inv_counts):
+def conv_forward(pn, feats, w, w_two, cot, proj, masks, sel, hot_t, inv_counts):
     half = MEMBERS // 2
     dma = pltpu.SemaphoreType.DMA
     vmem = pl.BlockSpec(memory_space=pltpu.VMEM)
@@ -434,7 +440,7 @@
             shape((pn.px, pn.width), BF16),
             shape((pn.C, pn.R, pn.piece, pn.width), BF16),
         ),
-        in_specs=[hbm, hbm, hbm, hbm, pl.BlockSpec(memory_space=pltpu.SMEM), vmem, vmem, vmem],
+        in_specs=[hbm, hbm, hbm, hbm, hbm, pl.BlockSpec(memory_space=pltpu.SMEM), vmem, vmem, vmem],
         out_specs=(vmem, hbm, hbm, vmem, vmem, vmem, vmem),
         scratch_shapes=[
             pltpu.VMEM((pn.nb * pn.rpb, pn.C * pn.bp, pn.cs), BF16),
@@ -453,7 +459,7 @@
         ],
         compiler_params=pltpu.CompilerParams(collective_id=0, has_side_effects=True, vmem_limit_bytes=60 * 2**20),
         name="conv_forward",
-    )(feats, w, cot, proj, masks, sel, hot_t, inv_counts)
+    )(feats, w, w_two, cot, proj, masks, sel, hot_t, inv_counts)
 
 
 def norm_kernel(pn, p, p4_in, gains, biases, valid, pixels, w_proj, cot, hot, hot_t, sel_t,
@@ -643,9 +649,9 @@
     )(p, p4, gains, biases, valid, pixels, w_proj, cot, hot, hot_t, sel_t)
 
 
-def back_kernel(pn, q_in, x_in, w_in, dproj_in, q4, means, hot_px, inv_counts, masks, lane_masks, shifts, sel_t,
+def back_kernel(pn, q_in, x_in, w_in, dproj_in, q4, means, hot_rows, inv_counts, masks, lane_masks, shifts, sel_t,
                 dw_out, dx_out, dproj_out,
-                xs, wbuf, qraw, qs, qt, dxe, dwbuf, inn, hsend, hrecv, pack, dp1, dps, dp2, dpf,
+                xs, wbuf, qraw, qs, qt, dxe, dwbuf, inn, hsend, hrecv, pack, pooled_rows, dp1, dps, dp2, dpf,
                 l_s, q_s, q_r, k_s, k_r, f_s, f_r, n_s, n_r, e_s, e_r, g_s, g_r, b_s, b_r, h_s, h_r, x_s, x_r,
                 p1_s, p1_r, p2_s, p2_r, p3_s, p3_r):
     row, col = lax.axis_index("row"), lax.axis_index("col")
@@ -1030,19 +1036,22 @@
     received(0)
     dwbuf[POOL] = dot_tn(means[...].astype(BF16), q4[...]).astype(BF16)
     dwbuf[POINT] = dot(qraw[0].T, xs[3, pl.ds(pn.hb * px, pn.own)]).T.astype(BF16)
-    dwbuf[TAPS - 1] = jnp.zeros((pn.cs, pn.width), BF16)
+    dwbuf[3 * GROUPS - 1] = jnp.zeros((pn.cs, pn.width), BF16)
     start_group(GROUPS - 1)
     late(GROUPS - 1, GROUPS)
     serve(4)
     pooled = dot_nt(q4[...], wbuf[POOL]) * inv_counts[...]
     pooled_high = pooled.astype(BF16)
     pooled_low = (pooled - pooled_high.astype(F32)).astype(BF16)
+    pooled_rows[...] = dot(hot_rows[...], pooled_high) + dot(hot_rows[...], pooled_low)
 
     def finish(rb, carry):
         at = pl.ds(pl.multiple_of(rb * many * px, 16), many * px)
         to = pl.ds(pl.multiple_of((rb * many + pn.hb) * px, 16), many * px)
-        hot = hot_px[at]
-        y = dot_nt(qraw[0, at], wbuf[POINT]) + dot(hot, pooled_high) + dot(hot, pooled_low)
+        y = dot_nt(qraw[0, at], wbuf[POINT])
+        y = jnp.concatenate(
+            [y[r * S:(r + 1) * S] + pooled_rows[pl.ds(rb * many * pn.rpb + r, 1)] for r in range(many * pn.rpb)], axis=0
+        )
         dxe[to] = dxe[to] + y
         return carry
 
@@ -1072,32 +1081,28 @@
         dxe[pl.ds(low, px)] = dxe[pl.ds(low, px)] + hrecv[0, pl.ds(rb * px, px)].astype(F32)
         dxe[pl.ds(high, px)] = dxe[pl.ds(high, px)] + hrecv[1, pl.ds(rb * px, px)].astype(F32)
 
-    def packing(rp, carry):
-        pair = dxe[pl.ds(pl.multiple_of(pn.hb * px + rp * 2 * S, 16), 2 * S)].astype(BF16)
-        pack[pl.ds(2 * rp, 2)] = dot(sel_t[...], pair).astype(BF16).reshape(2, pn.C * bp, pn.cs)
-        return carry
-
-    lax.fori_loop(0, H // 2, packing, 0, unroll=6)
+    column = lax.broadcasted_iota(jnp.int32, (S, pn.cs), 0).astype(F32)
+    for b in range(H // 8):
+        rows = []
+        for r in range(8 * b, 8 * b + 8):
+            values = dxe[pl.ds(pn.hb * px + r * S, S)]
+            rows.append(jnp.where(column < masks[6 * H + r], values, 0.0))
+        moved = dot(sel_t[...], jnp.concatenate(rows, axis=0).astype(BF16)).astype(BF16)
+        pack[8 * b // h, :, pl.ds(8 * b % h, 8)] = moved.reshape(pn.cols, 8, pn.cs)
+    own_lanes = pl.ds(pl.multiple_of(slice_of(pn, me) * pn.cs, 128), pn.cs)
     back = []
     for kk in range(1, MEMBERS):
         other = lax.rem(me + kk, MEMBERS)
         xo, co = other // pn.C, lax.rem(other, pn.C)
-        c = remote(pack.at[pl.ds(xo * h, h), pl.ds(pl.multiple_of(co * bp, bp), bp)], dx_out.at[slice_of(pn, me)], x_s.at[kk], x_r.at[kk],
+        c = remote(pack.at[xo, pl.ds(co * pn.bc, pn.bc)], dx_out.at[:, :, own_lanes], x_s.at[kk], x_r.at[kk],
                    member(slab, other))
         c.start()
         back.append(c)
-    c = pltpu.make_async_copy(pack.at[pl.ds(x * h, h), pl.ds(pl.multiple_of(col * bp, bp), bp)], dx_out.at[slice_of(pn, me)], x_r.at[0])
+    c = pltpu.make_async_copy(pack.at[x, pl.ds(col * pn.bc, pn.bc)], dx_out.at[:, :, own_lanes], x_r.at[0])
     c.start()
     back.append(c)
 
-    if pn.exchange:
-        done = 0
-        for g, end in ((6, 1), (7, 3), (8, 4), (9, 6), (10, 7), (11, 8), (None, GROUPS + 2)):
-            if g is not None:
-                serve(g)
-            lax.fori_loop(done, end, last_round, 0)
-            done = end
-
+    def close_dproj():
         @pl.when(slab == home_slab)
         def _():
             for z in range(n):
@@ -1115,6 +1120,16 @@
                 def _(c=c):
                     dproj_give(c).start()
 
+    if pn.exchange:
+        done = 0
+        for g, end in ((6, 1), (7, 3), (8, 4), (9, 6), (10, 7), (11, 8), (None, GROUPS + 2)):
+            if g is not None:
+                serve(g)
+            else:
+                close_dproj()
+            lax.fori_loop(done, end, last_round, 0)
+            done = end
+
         def settle(g, carry):
             early_links(g, lambda c: c.wait_send())
             late_links(g, lambda c: c.wait_send())
@@ -1167,19 +1182,19 @@
         c.wait()
 
 
-def conv_backward(pn, q, xs, w, dproj, q4, means, hot_px, inv_counts, masks, lane_masks, shifts, sel_t):
+def conv_backward(pn, q, xs, w, dproj, q4, means, hot_rows, inv_counts, masks, lane_masks, shifts, sel_t):
     dma = pltpu.SemaphoreType.DMA
     vmem = pl.BlockSpec(memory_space=pltpu.VMEM)
     hbm = pl.BlockSpec(memory_space=pl.ANY)
     shape = jax.ShapeDtypeStruct
     n = pn.slabs if pn.exchange else 1
-    sums = TAPS if pn.exchange else 1
+    sums = 3 * GROUPS if pn.exchange else 1
     block_rows = 5 * pn.width // MEMBERS
     return pl.pallas_call(
         functools.partial(back_kernel, pn),
         out_shape=(
-            shape((TAPS, pn.cs, pn.width), BF16),
-            shape((MEMBERS, pn.h, pn.bp, pn.cs), BF16),
+            shape((3 * GROUPS, pn.cs, pn.width), BF16),
+            shape((pn.bc, pn.h, pn.channels), BF16),
             shape((block_rows, pn.width), F32),
         ),
         in_specs=[hbm] * 4 + [vmem] * 4 + [pl.BlockSpec(memory_space=pltpu.SMEM)] + [vmem] * 3,
@@ -1191,11 +1206,12 @@
             pltpu.VMEM((3, 2, pn.own, pn.width), BF16),
             pltpu.VMEM((pn.width, pn.own), BF16),
             pltpu.VMEM((pn.ext, pn.cs), F32),
-            pltpu.VMEM((TAPS, pn.cs, pn.width), BF16),
+            pltpu.VMEM((3 * GROUPS, pn.cs, pn.width), BF16),
             pltpu.VMEM((2, sums, pn.cs, pn.width), BF16),
             pltpu.VMEM((2, pn.hb * pn.px, pn.cs), BF16),
             pltpu.VMEM((2, pn.hb * pn.px, pn.cs), BF16),
-            pltpu.VMEM((pn.H, pn.C * pn.bp, pn.cs), BF16),
+            pltpu.VMEM((pn.G, pn.cols, pn.h, pn.cs), BF16),
+            pltpu.VMEM((pn.H, pn.cs), F32),
             pltpu.VMEM((MEMBERS, block_rows, pn.width), BF16),
             pltpu.VMEM((block_rows, pn.width), BF16),
             pltpu.VMEM((n, block_rows, pn.width), BF16),
@@ -1208,7 +1224,7 @@
         ],
         compiler_params=pltpu.CompilerParams(collective_id=2, has_side_effects=True, vmem_limit_bytes=61900 * 1024),
         name="conv_backward",
-    )(q, xs, w, dproj, q4, means, hot_px, inv_counts, masks, lane_masks, shifts, sel_t)
+    )(q, xs, w, dproj, q4, means, hot_rows, inv_counts, masks, lane_masks, shifts, sel_t)
 
 
 def column_tables(pn):
@@ -1228,7 +1244,12 @@
                         shifts[b, n, r, c, r, s] = 1.0
     sel = sel.reshape(7 * 2 * S, 2 * pn.C * bp)
     sel_t = sel[3 * 2 * S:4 * 2 * S].T
-    return (jnp.asarray(sel, BF16), jnp.asarray(sel_t, BF16), jnp.asarray(shifts.reshape(12 * S, 2 * S), BF16))
+    sel_c = np.zeros((pn.cols, 8, 8, S), np.float32)
+    for c in range(pn.cols):
+        for r in range(8):
+            sel_c[c, r, r, c] = 1.0
+    sel_c = sel_c.reshape(8 * pn.cols, 8 * S)
+    return (jnp.asarray(sel, BF16), jnp.asarray(sel_t, BF16), jnp.asarray(sel_c, BF16), jnp.asarray(shifts.reshape(12 * S, 2 * S), BF16))
 
 
 def per_device(
@@ -1267,7 +1288,6 @@
     lane_masks = jnp.pad(jnp.repeat(same, pn.S, axis=1), ((0, 2), (0, 0))).astype(BF16)
     ncp_ids = jnp.arange(pn.ncp, dtype=jnp.int32)
     hot_rows = (mid[:, None] == ncp_ids[None, :]).astype(BF16)
-    hot_px = jnp.repeat(hot_rows, pn.S, axis=0)
     hot_t = jnp.repeat(hot_rows.T, pn.S, axis=1)
     inv_counts = jnp.pad(1.0 / counts, (0, pn.ncp - pn.crops))[:, None]
 
@@ -1278,35 +1298,36 @@
     block_hot = jnp.repeat((block_crop[:, None] == ncp_ids[None, :]).astype(BF16), pn.S, axis=0)
     block_hot_t = jnp.repeat((ncp_ids[:, None] == block_crop[None, :]).astype(BF16), pn.S, axis=1)
 
-    sel, sel_t, shifts = column_tables(pn)
-    none = jnp.zeros((1, *w_point.shape), BF16)
-    w = jnp.concatenate([w_atrous.transpose(1, 0, 2), w_point[None], w_pool[None], none], axis=0)
+    sel, sel_t, sel_c, shifts = column_tables(pn)
+    w, w_two = w_atrous.transpose(1, 0, 2), jnp.stack([w_point, w_pool])
     proj = w_proj.reshape(pn.C, pn.proj // pn.C, pn.width)
     proj = jnp.pad(proj, ((0, 0), (0, pn.piece - pn.proj // pn.C), (0, 0)))
     if not pn.exchange:
-        w = lax.all_gather(w, "row", axis=1, tiled=True)
+        w = lax.all_gather(jnp.concatenate([w, w_two], axis=0), "row", axis=1, tiled=True)
         w = lax.dynamic_slice_in_dim(w, slice_of(pn, x * pn.C + col) * pn.cs, pn.cs, axis=1)
-    flat = same.reshape(-1)
-    p, xs, w_own, means, p4, own_cot, pieces = conv_forward(pn, feats, w, cot, proj, flat, sel, hot_t, inv_counts)
+        w, w_two = w[:POINT], w[POINT:]
+    flat = jnp.concatenate([same.reshape(-1), widths_of(mid).astype(F32)])
+    p, xs, w_own, means, p4, own_cot, pieces = conv_forward(
+        pn, feats, w, w_two, cot, proj, flat, sel, hot_t, inv_counts
+    )
     full_proj = pieces[:, :, :pn.proj // pn.C].transpose(1, 0, 2, 3).reshape(5 * pn.width, pn.width)
     q, q4, d_proj, res, d_gains, d_biases = norms(
         pn, p, p4, gains, biases, valid, (1.0 / pixels)[None], full_proj, own_cot, block_hot, block_hot_t, sel_t
     )
     dw, dx, dproj_sum = conv_backward(
-        pn, q, xs, w_own, d_proj, q4, means, hot_px, inv_counts, flat, lane_masks, shifts, sel_t
+        pn, q, xs, w_own, d_proj, q4, means, hot_rows, inv_counts, flat, lane_masks, shifts, sel_c
     )
     if pn.exchange:
         d_proj = dproj_sum
     else:
-        whole = jnp.zeros((TAPS, channels, pn.width), BF16)
+        whole = jnp.zeros((3 * GROUPS, channels, pn.width), BF16)
         whole = lax.dynamic_update_slice(whole, dw, (0, slice_of(pn, x * pn.C + col) * pn.cs, 0))
         whole = lax.psum(whole, "col")
         dw = lax.psum_scatter(whole, "row", scatter_dimension=1, tiled=True)
         d_proj = lax.psum(d_proj, "col")
         d_proj = lax.psum_scatter(d_proj.astype(F32), "row", scatter_dimension=0, tiled=True)
     result = res[:, :bc]
-    dx = dx[:, :, :bc].transpose(1, 2, 0, 3).reshape(h, bc, channels)
-    d_features = jnp.where(own_valid[:, :, None], dx, 0)
+    d_features = dx.transpose(1, 0, 2)
     d_point = dw[POINT].astype(F32)
     d_atrous = dw[:POINT].astype(F32).transpose(1, 0, 2)
     d_pool = dw[POOL].astype(F32)

time: 313 us -> 302 us (0.965)
  local copies, waits for them, and re-layouts: 19.2 us -> 13.6 us
where the time goes in v2:
time: 302 us; the launch traced here: 299 us
  Pallas kernels  270 us (89%)
  other arithmetic  14.2 us (5%)
  local copies, waits for them, and re-layouts  13.6 us (5%)
    pallas_call x1, Pallas kernels, conv_backward(): pl.pallas_call(functools.partial(back_kernel, pn), out_shape=(shape((3 *...  133 us
    pallas_call x1, Pallas kernels, conv_forward(): pl.pallas_call(functools.partial(conv_kernel, pn), out_shape=(shape((4, p...  100 us
    pallas_call x1, Pallas kernels, norms(): pl.pallas_call(functools.partial(norm_kernel, pn), out_shape=(shape((4, p...  37 us

profile of v2, /device:TPU:9, one launch (start us, length us, event | category | flops | bytes accessed | tf_op | source)
XLA Modules:
  0.0 299.5 jit_solution(1383297511862188129)
XLA Ops:
  0.6 0.8 reduce-window.8
  1.5 0.1 convert_reduce_fusion.1
  1.6 0.7 select_reduce_fusion.2
  2.3 0.1 broadcast_compare_fusion
  2.4 1.5 broadcast_select_fusion
  3.9 0.4 copy.41
  4.2 0.8 copy.43
  5.0 0.0 copy-start.13
  5.1 1.4 pad.21.feats
  6.4 0.7 pad_maximum_fusion.w_two
  7.2 0.7 pad.22.cot
  7.9 0.6 pad.23.proj
  8.6 0.1 convert_reduce_fusion
  8.7 0.1 slice.37
  8.7 0.1 select_reduce_fusion.1
  8.8 0.1 compare_bitcast_fusion
  8.9 0.1 reshape.158
  9.0 0.7 pad_maximum_fusion.1.masks
  9.7 0.2 broadcast_in_dim.106
  9.9 0.9 reshape.153.hot_t
  10.7 0.6 convert_reduce_fusion.2
  11.3 0.7 copy.36.inv_counts
  12.0 100.1 %conv_forward.1 = (f32[4,336,256]{2,1,0:T(8,128)}, bf16[7,4704,256]{2,1,0:T(8,128)(2,1)}, bf16[29,256,256]{2,1,0:T(8,128)(2,1)}, f32[16,256]{1,0:T(8,128)}, f32[...) custom-call(bf16[8,24,16,256]{3,2,1,0:T(8,128)(2,1)} %pad.21.feats, ...), custom_call_target="tpu_custom_call" | custom-call | tf_op jit(solution)/shard_map/conv_forward/pallas_call | solution.py:432
  112.2 0.0 copy-start.4
  112.3 0.1 dynamic_slice.3
  112.3 0.2 select_reduce_fusion
  112.5 0.1 fusion.3
  112.6 0.1 reshape.162.valid
  113.4 1.1 slice_bitcast_fusion
  114.6 0.1 fusion.4
  114.7 0.1 broadcast_in_dim.112
  114.8 0.1 reshape.156.hot_t
  115.0 37.0 %norms.1 = (bf16[4,336,256]{2,1,0:T(8,128)(2,1)S(1)}, bf16[16,256]{1,0:T(8,128)(2,1)S(1)}, bf16[1280,256]{1,0:T(8,128)(2,1)S(1)}, bf16[24,16,256]{2,1,0:T(8,128)...) custom-call(f32[4,336,256]{2,1,0:T(8,128)S(1)} %copy-done, f32[16,256]{1,0:T(8,128)S(1)} %copy-done.5, ...), custom_call_target="tpu_custom_call" | custom-call | tf_op jit(solution)/shard_map/norms/pallas_call | solution.py:625
  152.0 0.8 copy-done.1
  152.8 0.8 copy-done.2
  153.7 0.7 copy.40
  154.4 0.7 fusion.hot_rows
  155.1 0.1 broadcast_in_dim.113
  155.2 0.2 reshape.157
  155.3 0.6 pad.25.lane_masks
  156.0 132.6 %conv_backward.1 = (bf16[30,256,256]{2,1,0:T(8,128)(2,1)}, bf16[13,24,2048]{2,1,0:T(8,128)(2,1)}, f32[160,256]{1,0:T(8,128)}) custom-call(bf16[4,336,256]{2,1,0:T(8,128)(2,1)} %copy-done.1, bf16[7,4704,256]{2,1,0:T(8,128)(2,1)} %get-tuple-element.30.x_in, bf16[29,256,256]{2,1,0:T(8,128)(2,1)} %get-tuple-element.31.w_in, bf16[1280,256]{1,0:T(8,128)(2,1)} %copy-done.2, ...), custom_call_target="tpu_custom_call" | custom-call | tf_op jit(solution)/shard_map/conv_backward/pallas_call | solution.py:1193
  288.6 1.8 bitcast_convert_fusion
  290.4 5.9 %convert_bitcast_fusion = f32[256,27,256]{2,0,1:T(8,128)} fusion(bf16[30,256,256]{2,1,0:T(8,128)(2,1)} %get-tuple-element.36), kind=kLoop, calls=%fused_computation | loop fusion | flops 1769472 | bytes 10616832 | tf_op jit(solution)/shard_map/transpose | solution.py:1332
  296.3 1.0 copy.48
  297.4 0.0 copy-done.10
  297.4 0.7 copy.49
  298.0 0.6 copy.50
  298.6 0.6 copy.51
  (43 shorter events, 0.3 us)
Async XLA Ops:
  5.0 1.4 copy-start.12
  5.0 1.4 copy-start.13
  5.0 2.1 copy-start.11
  5.0 2.9 copy-start.14
  5.1 3.7 %copy-start.16 = (s32[5]{0:T(128)S(1)}, s32[5]{0:T(128)}, u32[]{:S(2)}) copy-start(s32[5]{0:T(128)} %param.16) | copy-start | bytes 64
  6.4 4.3 %copy-start.15 = (s32[5]{0:T(128)S(1)}, s32[5]{0:T(128)}, u32[]{:S(2)}) copy-start(s32[5]{0:T(128)} %param.15) | copy-start | bytes 64
  112.2 2.7 copy-start
  112.2 2.7 copy-start.3
  112.2 2.7 copy-start.4
  112.2 2.7 copy-start.5
  112.2 2.7 copy-start.6
  112.2 2.7 copy-start.7
  152.0 0.8 copy-start.1
  152.8 0.8 copy-start.2
  153.7 0.7 copy-start.8
  290.4 6.0 %copy-start.9 = (bf16[13,24,2048]{2,1,0:T(8,128)(2,1)S(1)}, bf16[13,24,2048]{2,1,0:T(8,128)(2,1)}, u32[]{:S(2)}) copy-start(bf16[13,24,2048]{2,1,0:T(8,128)(2,1)} %get-tuple-element.35) | copy-start | bytes 3833860
  296.3 1.1 copy-start.10

commit v3 on v2

--- a/solution.py
+++ b/solution.py
@@ -14,6 +14,7 @@
 MEMBERS = 8
 TAPS = 29
 POINT, POOL, GROUPS = 27, 28, 10
+YIELD = 8
 MESH = pl.DeviceIdType.MESH
 F32 = jnp.float32
 BF16 = jnp.bfloat16
@@ -282,12 +283,19 @@
     begin(GROUPS - 1, 0)
     lax.fori_loop(early, GROUPS - 1, begin, 0)
 
+    column = lax.broadcasted_iota(jnp.int32, (pn.S, pn.cs), 0).astype(F32)
+
     def assemble(rp, carry):
         pair = ring[pl.ds(2 * rp, 2)].reshape(2 * pn.C * bp, pn.cs)
-        moved = dot(sel[...], pair).astype(BF16)
+        moved = dot(sel[...], pair)
         at = pl.multiple_of(rp * 2 * pn.S, 16)
+        wide = [masks[6 * H + 2 * rp + r] for r in range(2)]
         for v in range(7):
-            xs[v, pl.ds(at, 2 * pn.S)] = moved[v * 2 * pn.S:(v + 1) * 2 * pn.S]
+            rows = [
+                jnp.where(column + float(DILATIONS[0] * (v - 3)) < wide[r], moved[(2 * v + r) * pn.S:(2 * v + r + 1) * pn.S], 0.0)
+                for r in range(2)
+            ]
+            xs[v, pl.ds(at, 2 * pn.S)] = jnp.concatenate(rows, axis=0).astype(BF16)
         return carry
 
     lax.fori_loop(MARGIN // 2, (MARGIN + H) // 2, assemble, 0, unroll=6)
@@ -652,7 +660,7 @@
 def back_kernel(pn, q_in, x_in, w_in, dproj_in, q4, means, hot_rows, inv_counts, masks, lane_masks, shifts, sel_t,
                 dw_out, dx_out, dproj_out,
                 xs, wbuf, qraw, qs, qt, dxe, dwbuf, inn, hsend, hrecv, pack, pooled_rows, dp1, dps, dp2, dpf,
-                l_s, q_s, q_r, k_s, k_r, f_s, f_r, n_s, n_r, e_s, e_r, g_s, g_r, b_s, b_r, h_s, h_r, x_s, x_r,
+                l_s, q_s, q_r, k_s, k_r, f_s, f_r, n_s, n_r, e_s, e_r, g_s, g_r, b_s, b_r, turn_sem, h_s, h_r, x_s, x_r,
                 p1_s, p1_r, p2_s, p2_r, p3_s, p3_r):
     row, col = lax.axis_index("row"), lax.axis_index("col")
     slab, x = row // pn.G, lax.rem(row, pn.G)
@@ -672,6 +680,7 @@
     load_w.start()
     greet_all(pn, row, col)
 
+    slots = (1, 2, 3, 0)
     own_px = pl.ds(pl.multiple_of(me * px, 16), px)
     along_y, along_x = (row, lax.rem(col + 2, pn.C)), (slab * pn.G + lax.rem(x + 1, pn.G), col)
     from_y = x * pn.C + lax.rem(col + 2, pn.C)
@@ -688,6 +697,8 @@
         return remote(q_in.at[slot], qraw.at[slot, own_px], q_s.at[slot, 1], q_r.at[slot, 1], along_x)
 
     def on_to_x(slot):
+        if slot == slots[0]:
+            return remote(q_in.at[slot], qraw.at[slot, own_px], q_s.at[slot, 2], q_r.at[slot, 2], member(slab, from_xy))
         return remote(block_of(slot, from_y), block_of(slot, from_y), q_s.at[slot, 2], q_r.at[slot, 2], along_x)
 
     def to_partner(slot):
@@ -700,12 +711,12 @@
     def kept(slot):
         return pltpu.make_async_copy(q_in.at[slot], qraw.at[slot, own_px], l_s.at[2 + slot])
 
-    slots = (1, 2, 3, 0)
+    to_x(slots[0]).start()
+    on_to_x(slots[0]).start()
     for slot in slots:
         to_y(slot).start()
         to_partner(slot).start()
         kept(slot).start()
-    to_x(slots[0]).start()
 
     block_rows = 5 * pn.width // MEMBERS
     home_slab = me // pn.G
@@ -733,7 +744,8 @@
 
     def receive_y(slot):
         to_y(slot).wait()
-        on_to_x(slot).start()
+        if slot != slots[0]:
+            on_to_x(slot).start()
         passed(slot, 0).start()
         if slot != slots[-1]:
             to_x(slots[slots.index(slot) + 1]).start()
@@ -755,10 +767,11 @@
     first = (slab == 0) | (slab == n - 1)
     half_rows = pn.cs // 2
     detour_up, detour_down = (slab == 0) & (col == 2), (slab == n - 1) & (col == 3)
+    yielding = first & jnp.logical_not(closing | detour_up | detour_down)
     relay_up, relay_down = (slab == 0) & (col == 0), (slab == n - 1) & (col == 1)
 
     def taps(g):
-        return pl.ds(3 * g, 3)
+        return pl.ds(POINT, 2) if isinstance(g, int) and g == GROUPS - 1 else pl.ds(3 * g, 3)
 
     def part_of(ref, g, half):
         return ref.at[taps(g), pl.ds(half * half_rows, half_rows)]
@@ -859,27 +872,29 @@
                 ).astype(BF16)
                 share(g, 1, part_of(inn.at[side], g, 1))
 
-    def relay_many(start, end):
-        def one(g, carry):
-            for role, up in ((relay_up, True), (relay_down, False)):
-                @pl.when(role)
-                def _(up=up):
+    def give_way():
+        @pl.when(yielding)
+        def _():
+            for g in range(YIELD):
+                early_links(g, lambda c: c.wait_send())
+            pl.semaphore_signal(turn_sem, inc=1, device_id=partner, device_id_type=MESH)
+
+        @pl.when(detour_up | detour_down)
+        def _():
+            pl.semaphore_wait(turn_sem, 1)
+
+        for g in range(GROUPS):
+            late_links(g, lambda c: c.start())
+
+    def relay_all():
+        for role, up in ((relay_up, True), (relay_down, False)):
+            @pl.when(role)
+            def _(up=up):
+                pl.semaphore_wait(turn_sem, 1)
+                for g in range(GROUPS):
                     at = part_of(inn.at[0 if up else 1], g, 1)
                     pltpu.make_async_copy(at, at, e_r.at[g]).wait()
                     relay(g, up).start()
-            return carry
-
-        if pn.exchange:
-            lax.fori_loop(start, end, one, 0)
-
-    def late(start, end):
-        def one(g, carry):
-            late_links(g, lambda c: c.start())
-            return carry
-
-        if pn.exchange:
-            lax.fori_loop(start, end, one, 0)
-        relay_many(start, end)
 
     def pass_on(g):
         for going, up in ((rising, True), (falling, False)):
@@ -908,21 +923,15 @@
             close(g - 2)
             from_far(g - 2)
 
-    def last_round(g, carry):
-        @pl.when(g < GROUPS)
-        def _():
+    def last_round(g):
+        if g < GROUPS:
             close_half(g)
-
-        @pl.when(g > 1)
-        def _():
-            before = jnp.maximum(g - 2, 0)
+        if g > 1:
             for half, role in ((0, end_getting | close_b), (1, end_getting | close_a)):
                 @pl.when(role)
                 def _(half=half):
-                    landed(before, half)
-                    share_on(before, half).start()
-
-        return carry
+                    landed(g - 2, half)
+                    share_on(g - 2, half).start()
 
     def start_group(g):
         if not pn.exchange:
@@ -1013,7 +1022,6 @@
 
     for g in (6, 7, 8):
         start_group(g)
-    late(0, GROUPS - 1)
     serve(3)
 
     if pn.exchange:
@@ -1036,9 +1044,7 @@
     received(0)
     dwbuf[POOL] = dot_tn(means[...].astype(BF16), q4[...]).astype(BF16)
     dwbuf[POINT] = dot(qraw[0].T, xs[3, pl.ds(pn.hb * px, pn.own)]).T.astype(BF16)
-    dwbuf[3 * GROUPS - 1] = jnp.zeros((pn.cs, pn.width), BF16)
     start_group(GROUPS - 1)
-    late(GROUPS - 1, GROUPS)
     serve(4)
     pooled = dot_nt(q4[...], wbuf[POOL]) * inv_counts[...]
     pooled_high = pooled.astype(BF16)
@@ -1056,6 +1062,8 @@
         return carry
 
     lax.fori_loop(0, MEMBERS // many, finish, 0)
+    if pn.exchange:
+        relay_all()
     serve(5)
 
     @pl.when(slab > 0)
@@ -1086,7 +1094,7 @@
         rows = []
         for r in range(8 * b, 8 * b + 8):
             values = dxe[pl.ds(pn.hb * px + r * S, S)]
-            rows.append(jnp.where(column < masks[6 * H + r], values, 0.0))
+            rows.append(jnp.where(column < masks[6 * H + MARGIN + r], values, 0.0))
         moved = dot(sel_t[...], jnp.concatenate(rows, axis=0).astype(BF16)).astype(BF16)
         pack[8 * b // h, :, pl.ds(8 * b % h, 8)] = moved.reshape(pn.cols, 8, pn.cs)
     own_lanes = pl.ds(pl.multiple_of(slice_of(pn, me) * pn.cs, 128), pn.cs)
@@ -1121,17 +1129,20 @@
                     dproj_give(c).start()
 
     if pn.exchange:
-        done = 0
-        for g, end in ((6, 1), (7, 3), (8, 4), (9, 6), (10, 7), (11, 8), (None, GROUPS + 2)):
-            if g is not None:
-                serve(g)
-            else:
-                close_dproj()
-            lax.fori_loop(done, end, last_round, 0)
-            done = end
+        serve(6)
+        serve(7)
+        give_way()
+        for g in range(8, GROUPS + 2):
+            serve(g)
+        close_dproj()
+        for g in range(GROUPS + 2):
+            last_round(g)
 
         def settle(g, carry):
-            early_links(g, lambda c: c.wait_send())
+            @pl.when(jnp.logical_not(yielding & (g < YIELD)))
+            def _():
+                early_links(g, lambda c: c.wait_send())
+
             late_links(g, lambda c: c.wait_send())
             for role, up in ((relay_up, True), (relay_down, False)):
                 @pl.when(role)
@@ -1159,7 +1170,8 @@
 
             return carry
 
-        lax.fori_loop(0, GROUPS, settle, 0)
+        lax.fori_loop(0, GROUPS - 1, settle, 0)
+        settle(GROUPS - 1, 0)
 
         @pl.when(slab != home_slab)
         def _():
@@ -1188,12 +1200,12 @@
     hbm = pl.BlockSpec(memory_space=pl.ANY)
     shape = jax.ShapeDtypeStruct
     n = pn.slabs if pn.exchange else 1
-    sums = 3 * GROUPS if pn.exchange else 1
+    sums = TAPS if pn.exchange else 1
     block_rows = 5 * pn.width // MEMBERS
     return pl.pallas_call(
         functools.partial(back_kernel, pn),
         out_shape=(
-            shape((3 * GROUPS, pn.cs, pn.width), BF16),
+            shape((TAPS, pn.cs, pn.width), BF16),
             shape((pn.bc, pn.h, pn.channels), BF16),
             shape((block_rows, pn.width), F32),
         ),
@@ -1206,7 +1218,7 @@
             pltpu.VMEM((3, 2, pn.own, pn.width), BF16),
             pltpu.VMEM((pn.width, pn.own), BF16),
             pltpu.VMEM((pn.ext, pn.cs), F32),
-            pltpu.VMEM((3 * GROUPS, pn.cs, pn.width), BF16),
+            pltpu.VMEM((TAPS, pn.cs, pn.width), BF16),
             pltpu.VMEM((2, sums, pn.cs, pn.width), BF16),
             pltpu.VMEM((2, pn.hb * pn.px, pn.cs), BF16),
             pltpu.VMEM((2, pn.hb * pn.px, pn.cs), BF16),
@@ -1218,7 +1230,7 @@
             pltpu.VMEM((block_rows, pn.width), F32),
             dma((6,)), dma((4, 3)), dma((4, 3)), dma((4,)), dma((4,)), dma((4, 3)), dma((4, 3)),
             dma((2, GROUPS)), dma((2, 2, GROUPS)), dma((GROUPS,)), dma((GROUPS,)), dma((2, 2, GROUPS)), dma((2, GROUPS)),
-            dma((GROUPS,)), dma((GROUPS,)),
+            dma((GROUPS,)), dma((GROUPS,)), pltpu.SemaphoreType.REGULAR,
             dma((2,)), dma((2,)), dma((MEMBERS,)), dma((MEMBERS,)),
             dma((MEMBERS,)), dma((MEMBERS,)), dma((1,)), dma((n,)), dma((pn.C,)), dma((1,)),
         ],
@@ -1271,11 +1283,7 @@
     def widths_of(crop):
         return jnp.sum(jnp.where(crop[:, None] == crop_ids[None, :], crop_cols[None, :], 0), axis=1)
 
-    own_crop = crop_of(row * h + jnp.arange(h, dtype=jnp.int32))
-    own_columns = col * bc + jnp.arange(bc, dtype=jnp.int32)
-    own_valid = own_columns[None, :] < widths_of(own_crop)[:, None]
-    masked = jnp.where(own_valid[:, :, None], features, 0)
-    feats = masked.reshape(h, bc, MEMBERS, pn.cs).transpose(2, 0, 1, 3)
+    feats = features.reshape(h, bc, MEMBERS, pn.cs).transpose(2, 0, 1, 3)
     feats = jnp.pad(feats, ((0, 0), (0, 0), (0, pn.bp - bc), (0, 0)))
     cot = jnp.pad(cotangent, ((0, 0), (0, pn.bp - bc), (0, 0)))
 
@@ -1306,7 +1314,7 @@
         w = lax.all_gather(jnp.concatenate([w, w_two], axis=0), "row", axis=1, tiled=True)
         w = lax.dynamic_slice_in_dim(w, slice_of(pn, x * pn.C + col) * pn.cs, pn.cs, axis=1)
         w, w_two = w[:POINT], w[POINT:]
-    flat = jnp.concatenate([same.reshape(-1), widths_of(mid).astype(F32)])
+    flat = jnp.concatenate([same.reshape(-1), widths_of(crops).astype(F32)])
     p, xs, w_own, means, p4, own_cot, pieces = conv_forward(
         pn, feats, w, w_two, cot, proj, flat, sel, hot_t, inv_counts
     )
@@ -1320,7 +1328,7 @@
     if pn.exchange:
         d_proj = dproj_sum
     else:
-        whole = jnp.zeros((3 * GROUPS, channels, pn.width), BF16)
+        whole = jnp.zeros((TAPS, channels, pn.width), BF16)
         whole = lax.dynamic_update_slice(whole, dw, (0, slice_of(pn, x * pn.C + col) * pn.cs, 0))
         whole = lax.psum(whole, "col")
         dw = lax.psum_scatter(whole, "row", scatter_dimension=1, tiled=True)

time: 302 us -> 299 us (0.990)
    pallas_call x1, Pallas kernels: 133 us -> 130 us  [conv_backward(): pl.pallas_call(functools.partial(back_kernel, pn), out_shape=(shape((TAPS...]
where the time goes in v3:
time: 299 us; the launch traced here: 296 us
  Pallas kernels  267 us (89%)
  local copies, waits for them, and re-layouts  16.5 us (6%)
  other arithmetic  11.2 us (4%)
    pallas_call x1, Pallas kernels, conv_backward(): pl.pallas_call(functools.partial(back_kernel, pn), out_shape=(shape((TAPS...  130 us
    pallas_call x1, Pallas kernels, conv_forward(): pl.pallas_call(functools.partial(conv_kernel, pn), out_shape=(shape((4, p...  100 us
    pallas_call x1, Pallas kernels, norms(): pl.pallas_call(functools.partial(norm_kernel, pn), out_shape=(shape((4, p...  37 us
    unnamed x41, local copies, waits for them, and re-layouts  8.71 us

profile of v3, /device:TPU:9, one launch (start us, length us, event | category | flops | bytes accessed | tf_op | source)
XLA Modules:
  0.0 296.2 jit_solution(15899494757443467673)
XLA Ops:
  0.6 1.7 copy.41
  2.3 0.0 copy-start.12
  2.3 0.0 copy-start.13
  2.4 0.0 copy-start.15
  2.4 0.0 copy-start.16
  2.4 0.8 copy.43
  3.2 1.4 pad.21.feats
  4.5 0.7 pad_maximum_fusion.w_two
  5.3 0.7 pad.22.cot
  6.0 0.6 pad.23.proj
  6.6 0.2 reduce-window.8
  6.8 0.1 convert_reduce_fusion
  6.9 0.1 select_reduce_fusion.1
  7.0 0.1 compare_bitcast_fusion
  7.1 0.1 reshape.122
  7.2 0.6 pad_maximum_fusion.1.masks
  7.8 0.1 slice.37
  7.9 0.2 broadcast_in_dim.65
  8.1 0.9 reshape.117.hot_t
  8.9 0.6 convert_reduce_fusion.1
  9.6 0.7 copy.36.inv_counts
  10.2 100.2 %conv_forward.1 = (f32[4,336,256]{2,1,0:T(8,128)}, bf16[7,4704,256]{2,1,0:T(8,128)(2,1)}, bf16[29,256,256]{2,1,0:T(8,128)(2,1)}, f32[16,256]{1,0:T(8,128)}, f32[...) custom-call(bf16[8,24,16,256]{3,2,1,0:T(8,128)(2,1)} %pad.21.feats, ...), custom_call_target="tpu_custom_call" | custom-call | tf_op jit(solution)/shard_map/conv_forward/pallas_call | solution.py:440
  110.5 0.1 dynamic_slice.3
  110.5 0.2 select_reduce_fusion
  110.7 0.1 fusion.3
  110.8 0.1 reshape.126.valid
  111.6 1.1 slice_bitcast_fusion
  112.8 0.1 fusion.4
  112.9 0.1 broadcast_in_dim.71
  113.0 0.1 reshape.120.hot_t
  113.1 0.9 copy-done.3
  114.1 0.7 copy-done.5
  114.8 37.0 %norms.1 = (bf16[4,336,256]{2,1,0:T(8,128)(2,1)S(1)}, bf16[16,256]{1,0:T(8,128)(2,1)S(1)}, bf16[1280,256]{1,0:T(8,128)(2,1)S(1)}, bf16[24,16,256]{2,1,0:T(8,128)...) custom-call(f32[4,336,256]{2,1,0:T(8,128)S(1)} %copy-done, f32[16,256]{1,0:T(8,128)S(1)} %copy-done.5, ...), custom_call_target="tpu_custom_call" | custom-call | tf_op jit(solution)/shard_map/norms/pallas_call | solution.py:633
  151.8 0.0 copy-start.1
  151.8 0.8 copy-done.1
  152.6 0.8 copy-done.2
  153.4 0.7 copy.40
  154.2 0.7 fusion.hot_rows
  154.8 0.1 broadcast_in_dim.72
  154.9 0.2 reshape.121
  155.1 0.6 pad.25.lane_masks
  155.7 129.6 %conv_backward.1 = (bf16[29,256,256]{2,1,0:T(8,128)(2,1)}, bf16[13,24,2048]{2,1,0:T(8,128)(2,1)}, f32[160,256]{1,0:T(8,128)}) custom-call(bf16[4,336,256]{2,1,0:T(8,128)(2,1)} %copy-done.1, bf16[7,4704,256]{2,1,0:T(8,128)(2,1)} %get-tuple-element.30.x_in, bf16[29,256,256]{2,1,0:T(8,128)(2,1)} %get-tuple-element.31.w_in, bf16[1280,256]{1,0:T(8,128)(2,1)} %copy-done.2, ...), custom_call_target="tpu_custom_call" | custom-call | tf_op jit(solution)/shard_map/conv_backward/pallas_call | solution.py:1205
  285.3 1.8 bitcast_convert_fusion
  287.1 6.0 %convert_bitcast_fusion = f32[256,27,256]{2,0,1:T(8,128)} fusion(bf16[29,256,256]{2,1,0:T(8,128)(2,1)} %get-tuple-element.36), kind=kLoop, calls=%fused_computation | loop fusion | flops 1769472 | bytes 10616832 | tf_op jit(solution)/shard_map/transpose | solution.py:1340
  293.1 1.0 copy.48
  294.1 0.7 copy.49
  294.8 0.6 copy.50
  295.4 0.6 copy.51
  (36 shorter events, 0.2 us)
Async XLA Ops:
  2.3 2.2 copy-start.12
  2.3 2.2 copy-start.13
  2.3 2.9 copy-start.11
  2.4 3.6 %copy-start.14 = (bf16[160,256]{1,0:T(8,128)(2,1)S(1)}, bf16[160,256]{1,0:T(8,128)(2,1)}, u32[]{:S(2)}) copy-start(bf16[160,256]{1,0:T(8,128)(2,1)} %param.20) | copy-start | bytes 245764
  2.4 4.3 %copy-start.15 = (s32[5]{0:T(128)S(1)}, s32[5]{0:T(128)}, u32[]{:S(2)}) copy-start(s32[5]{0:T(128)} %param.15) | copy-start | bytes 64
  2.4 4.5 %copy-start.16 = (s32[5]{0:T(128)S(1)}, s32[5]{0:T(128)}, u32[]{:S(2)}) copy-start(s32[5]{0:T(128)} %param.16) | copy-start | bytes 64
  10.2 102.9 %copy-start.4 = (bf16[128,112]{1,0:T(8,128)(2,1)S(1)}, bf16[128,112]{1,0:T(8,128)(2,1)}, u32[]{:S(2)}) copy-start(bf16[128,112]{1,0:T(8,128)(2,1)} %constant.66.clone.sel_t) | copy-start | bytes 86020
  10.2 102.9 %copy-start.6 = (f32[6,256]{1,0:T(8,128)S(1)}, f32[6,256]{1,0:T(8,128)}, u32[]{:S(2)}) copy-start(f32[6,256]{1,0:T(8,128)} %gains.1) | copy-start | bytes 18436
  10.2 102.9 %copy-start.7 = (f32[6,256]{1,0:T(8,128)S(1)}, f32[6,256]{1,0:T(8,128)}, u32[]{:S(2)}) copy-start(f32[6,256]{1,0:T(8,128)} %biases.1) | copy-start | bytes 18436
  110.4 2.7 copy-start
  113.1 0.9 copy-start.3
  114.1 0.7 copy-start.5
  151.8 0.8 copy-start.1
  152.6 0.8 copy-start.2
  153.4 0.7 copy-start.8
  287.1 6.0 %copy-start.9 = (bf16[13,24,2048]{2,1,0:T(8,128)(2,1)S(1)}, bf16[13,24,2048]{2,1,0:T(8,128)(2,1)}, u32[]{:S(2)}) copy-start(bf16[13,24,2048]{2,1,0:T(8,128)(2,1)} %get-tuple-element.35) | copy-start | bytes 3833860
  287.1 7.0 %copy-start.10 = (f32[160,256]{1,0:T(8,128)S(1)}, f32[160,256]{1,0:T(8,128)}, u32[]{:S(2)}) copy-start(f32[160,256]{1,0:T(8,128)} %get-tuple-element.89) | copy-start | bytes 491524

commit v4 on v3

--- a/solution.py
+++ b/solution.py
@@ -896,9 +896,11 @@
                     pltpu.make_async_copy(at, at, e_r.at[g]).wait()
                     relay(g, up).start()
 
-    def pass_on(g):
+    def pass_on(g, hop):
         for going, up in ((rising, True), (falling, False)):
-            @pl.when(going & jnp.logical_not(first))
+            at_hop = (slab == 1) if up == (hop == 1) else (slab != 1)
+
+            @pl.when(going & jnp.logical_not(first) & at_hop)
             def _(up=up):
                 arrived(g, 0 if up else 1)
                 add(g, 0 if up else 1)
@@ -918,7 +920,9 @@
         if not pn.exchange:
             return
         if g < GROUPS:
-            pass_on(g)
+            pass_on(g, 1)
+        if 0 < g <= GROUPS:
+            pass_on(g - 1, 2)
         if g > 1:
             close(g - 2)
             from_far(g - 2)

time: 299 us -> 299 us (level)
  no operation moved by 1% of the time
where the time goes in v4:
time: 299 us; the launch traced here: 296 us
  Pallas kernels  267 us (89%)
  local copies, waits for them, and re-layouts  16.5 us (6%)
  other arithmetic  11.2 us (4%)
    pallas_call x1, Pallas kernels, conv_backward(): pl.pallas_call(functools.partial(back_kernel, pn), out_shape=(shape((TAPS...  130 us
    pallas_call x1, Pallas kernels, conv_forward(): pl.pallas_call(functools.partial(conv_kernel, pn), out_shape=(shape((4, p...  100 us
    pallas_call x1, Pallas kernels, norms(): pl.pallas_call(functools.partial(norm_kernel, pn), out_shape=(shape((4, p...  37 us
    unnamed x41, local copies, waits for them, and re-layouts  8.71 us

profile of v4, /device:TPU:9, one launch (start us, length us, event | category | flops | bytes accessed | tf_op | source)
XLA Modules:
  0.0 296.4 jit_solution(271877021574617840)
XLA Ops:
  0.6 1.7 copy.41
  2.3 0.0 copy-start.12
  2.3 0.0 copy-start.13
  2.4 0.0 copy-start.15
  2.4 0.0 copy-start.16
  2.4 0.8 copy.43
  3.2 1.4 pad.21.feats
  4.5 0.7 pad_maximum_fusion.w_two
  5.3 0.7 pad.22.cot
  6.0 0.6 pad.23.proj
  6.6 0.2 reduce-window.8
  6.8 0.1 convert_reduce_fusion
  6.9 0.1 select_reduce_fusion.1
  7.0 0.1 compare_bitcast_fusion
  7.1 0.1 reshape.122
  7.2 0.6 pad_maximum_fusion.1.masks
  7.8 0.1 slice.37
  7.9 0.2 broadcast_in_dim.65
  8.1 0.9 reshape.117.hot_t
  8.9 0.6 convert_reduce_fusion.1
  9.6 0.7 copy.36.inv_counts
  10.2 100.2 %conv_forward.1 = (f32[4,336,256]{2,1,0:T(8,128)}, bf16[7,4704,256]{2,1,0:T(8,128)(2,1)}, bf16[29,256,256]{2,1,0:T(8,128)(2,1)}, f32[16,256]{1,0:T(8,128)}, f32[...) custom-call(bf16[8,24,16,256]{3,2,1,0:T(8,128)(2,1)} %pad.21.feats, ...), custom_call_target="tpu_custom_call" | custom-call | tf_op jit(solution)/shard_map/conv_forward/pallas_call | solution.py:440
  110.5 0.1 dynamic_slice.3
  110.5 0.2 select_reduce_fusion
  110.7 0.1 fusion.3
  110.8 0.1 reshape.126.valid
  111.6 1.1 slice_bitcast_fusion
  112.8 0.1 fusion.4
  112.9 0.1 broadcast_in_dim.71
  113.0 0.1 reshape.120.hot_t
  113.1 0.9 copy-done.3
  114.1 0.7 copy-done.5
  114.8 37.0 %norms.1 = (bf16[4,336,256]{2,1,0:T(8,128)(2,1)S(1)}, bf16[16,256]{1,0:T(8,128)(2,1)S(1)}, bf16[1280,256]{1,0:T(8,128)(2,1)S(1)}, bf16[24,16,256]{2,1,0:T(8,128)...) custom-call(f32[4,336,256]{2,1,0:T(8,128)S(1)} %copy-done, f32[16,256]{1,0:T(8,128)S(1)} %copy-done.5, ...), custom_call_target="tpu_custom_call" | custom-call | tf_op jit(solution)/shard_map/norms/pallas_call | solution.py:633
  151.8 0.0 copy-start.1
  151.8 0.8 copy-done.1
  152.6 0.8 copy-done.2
  153.4 0.7 copy.40
  154.2 0.7 fusion.hot_rows
  154.8 0.1 broadcast_in_dim.72
  154.9 0.2 reshape.121
  155.1 0.6 pad.25.lane_masks
  155.7 129.8 %conv_backward.1 = (bf16[29,256,256]{2,1,0:T(8,128)(2,1)}, bf16[13,24,2048]{2,1,0:T(8,128)(2,1)}, f32[160,256]{1,0:T(8,128)}) custom-call(bf16[4,336,256]{2,1,0:T(8,128)(2,1)} %copy-done.1, bf16[7,4704,256]{2,1,0:T(8,128)(2,1)} %get-tuple-element.30.x_in, bf16[29,256,256]{2,1,0:T(8,128)(2,1)} %get-tuple-element.31.w_in, bf16[1280,256]{1,0:T(8,128)(2,1)} %copy-done.2, ...), custom_call_target="tpu_custom_call" | custom-call | tf_op jit(solution)/shard_map/conv_backward/pallas_call | solution.py:1209
  285.6 1.8 bitcast_convert_fusion
  287.4 6.0 %convert_bitcast_fusion = f32[256,27,256]{2,0,1:T(8,128)} fusion(bf16[29,256,256]{2,1,0:T(8,128)(2,1)} %get-tuple-element.36), kind=kLoop, calls=%fused_computation | loop fusion | flops 1769472 | bytes 10616832 | tf_op jit(solution)/shard_map/transpose | solution.py:1344
  293.3 1.0 copy.48
  294.4 0.7 copy.49
  295.0 0.6 copy.50
  295.6 0.6 copy.51
  (36 shorter events, 0.2 us)
Async XLA Ops:
  2.3 2.2 copy-start.12
  2.3 2.2 copy-start.13
  2.3 2.9 copy-start.11
  2.4 3.6 %copy-start.14 = (bf16[160,256]{1,0:T(8,128)(2,1)S(1)}, bf16[160,256]{1,0:T(8,128)(2,1)}, u32[]{:S(2)}) copy-start(bf16[160,256]{1,0:T(8,128)(2,1)} %param.20) | copy-start | bytes 245764
  2.4 4.3 %copy-start.15 = (s32[5]{0:T(128)S(1)}, s32[5]{0:T(128)}, u32[]{:S(2)}) copy-start(s32[5]{0:T(128)} %param.15) | copy-start | bytes 64
  2.4 4.5 %copy-start.16 = (s32[5]{0:T(128)S(1)}, s32[5]{0:T(128)}, u32[]{:S(2)}) copy-start(s32[5]{0:T(128)} %param.16) | copy-start | bytes 64
  10.2 102.9 %copy-start.4 = (bf16[128,112]{1,0:T(8,128)(2,1)S(1)}, bf16[128,112]{1,0:T(8,128)(2,1)}, u32[]{:S(2)}) copy-start(bf16[128,112]{1,0:T(8,128)(2,1)} %constant.66.clone.sel_t) | copy-start | bytes 86020
  10.2 102.9 %copy-start.6 = (f32[6,256]{1,0:T(8,128)S(1)}, f32[6,256]{1,0:T(8,128)}, u32[]{:S(2)}) copy-start(f32[6,256]{1,0:T(8,128)} %gains.1) | copy-start | bytes 18436
  10.2 102.9 %copy-start.7 = (f32[6,256]{1,0:T(8,128)S(1)}, f32[6,256]{1,0:T(8,128)}, u32[]{:S(2)}) copy-start(f32[6,256]{1,0:T(8,128)} %biases.1) | copy-start | bytes 18436
  110.4 2.7 copy-start
  113.1 0.9 copy-start.3
  114.1 0.7 copy-start.5
  151.8 0.8 copy-start.1
  152.6 0.8 copy-start.2
  153.4 0.7 copy-start.8
  287.4 6.0 %copy-start.9 = (bf16[13,24,2048]{2,1,0:T(8,128)(2,1)S(1)}, bf16[13,24,2048]{2,1,0:T(8,128)(2,1)}, u32[]{:S(2)}) copy-start(bf16[13,24,2048]{2,1,0:T(8,128)(2,1)} %get-tuple-element.35) | copy-start | bytes 3833860
  287.4 7.0 %copy-start.10 = (f32[160,256]{1,0:T(8,128)S(1)}, f32[160,256]{1,0:T(8,128)}, u32[]{:S(2)}) copy-start(f32[160,256]{1,0:T(8,128)} %get-tuple-element.89) | copy-start | bytes 491524

commit v5 on v3

--- a/solution.py
+++ b/solution.py
@@ -14,7 +14,7 @@
 MEMBERS = 8
 TAPS = 29
 POINT, POOL, GROUPS = 27, 28, 10
-YIELD = 8
+YIELD = 5
 MESH = pl.DeviceIdType.MESH
 F32 = jnp.float32
 BF16 = jnp.bfloat16

time: 299 us -> 306 us (1.023)
  Pallas kernels: 267 us -> 273 us
    pallas_call x1, Pallas kernels: 130 us -> 136 us  [conv_backward(): pl.pallas_call(functools.partial(back_kernel, pn), out_shape=(shape((TAPS...]
where the time goes in v5:
time: 306 us; the launch traced here: 303 us
  Pallas kernels  273 us (89%)
  local copies, waits for them, and re-layouts  16.5 us (5%)
  other arithmetic  11.2 us (4%)
    pallas_call x1, Pallas kernels, conv_backward(): pl.pallas_call(functools.partial(back_kernel, pn), out_shape=(shape((TAPS...  136 us
    pallas_call x1, Pallas kernels, conv_forward(): pl.pallas_call(functools.partial(conv_kernel, pn), out_shape=(shape((4, p...  100 us
    pallas_call x1, Pallas kernels, norms(): pl.pallas_call(functools.partial(norm_kernel, pn), out_shape=(shape((4, p...  37 us
    unnamed x41, local copies, waits for them, and re-layouts  8.71 us

profile of v5, /device:TPU:9, one launch (start us, length us, event | category | flops | bytes accessed | tf_op | source)
XLA Modules:
  0.0 302.7 jit_solution(2339117539694325718)
XLA Ops:
  0.6 1.7 copy.41
  2.3 0.0 copy-start.12
  2.3 0.0 copy-start.13
  2.4 0.0 copy-start.15
  2.4 0.0 copy-start.16
  2.4 0.8 copy.43
  3.2 1.4 pad.21.feats
  4.5 0.7 pad_maximum_fusion.w_two
  5.3 0.7 pad.22.cot
  6.0 0.6 pad.23.proj
  6.6 0.2 reduce-window.8
  6.8 0.1 convert_reduce_fusion
  6.9 0.1 select_reduce_fusion.1
  7.0 0.1 compare_bitcast_fusion
  7.1 0.1 reshape.122
  7.2 0.6 pad_maximum_fusion.1.masks
  7.8 0.1 slice.37
  7.9 0.2 broadcast_in_dim.65
  8.1 0.9 reshape.117.hot_t
  8.9 0.6 convert_reduce_fusion.1
  9.6 0.7 copy.36.inv_counts
  10.2 100.2 %conv_forward.1 = (f32[4,336,256]{2,1,0:T(8,128)}, bf16[7,4704,256]{2,1,0:T(8,128)(2,1)}, bf16[29,256,256]{2,1,0:T(8,128)(2,1)}, f32[16,256]{1,0:T(8,128)}, f32[...) custom-call(bf16[8,24,16,256]{3,2,1,0:T(8,128)(2,1)} %pad.21.feats, ...), custom_call_target="tpu_custom_call" | custom-call | tf_op jit(solution)/shard_map/conv_forward/pallas_call | solution.py:440
  110.5 0.1 dynamic_slice.3
  110.5 0.2 select_reduce_fusion
  110.7 0.1 fusion.3
  110.8 0.1 reshape.126.valid
  111.6 1.1 slice_bitcast_fusion
  112.8 0.1 fusion.4
  112.9 0.1 broadcast_in_dim.71
  113.0 0.1 reshape.120.hot_t
  113.1 0.9 copy-done.3
  114.1 0.7 copy-done.5
  114.8 37.0 %norms.1 = (bf16[4,336,256]{2,1,0:T(8,128)(2,1)S(1)}, bf16[16,256]{1,0:T(8,128)(2,1)S(1)}, bf16[1280,256]{1,0:T(8,128)(2,1)S(1)}, bf16[24,16,256]{2,1,0:T(8,128)...) custom-call(f32[4,336,256]{2,1,0:T(8,128)S(1)} %copy-done, f32[16,256]{1,0:T(8,128)S(1)} %copy-done.5, ...), custom_call_target="tpu_custom_call" | custom-call | tf_op jit(solution)/shard_map/norms/pallas_call | solution.py:633
  151.8 0.0 copy-start.1
  151.8 0.8 copy-done.1
  152.6 0.8 copy-done.2
  153.4 0.7 copy.40
  154.2 0.7 fusion.hot_rows
  154.8 0.1 broadcast_in_dim.72
  154.9 0.2 reshape.121
  155.1 0.6 pad.25.lane_masks
  155.7 136.1 %conv_backward.1 = (bf16[29,256,256]{2,1,0:T(8,128)(2,1)}, bf16[13,24,2048]{2,1,0:T(8,128)(2,1)}, f32[160,256]{1,0:T(8,128)}) custom-call(bf16[4,336,256]{2,1,0:T(8,128)(2,1)} %copy-done.1, bf16[7,4704,256]{2,1,0:T(8,128)(2,1)} %get-tuple-element.30.x_in, bf16[29,256,256]{2,1,0:T(8,128)(2,1)} %get-tuple-element.31.w_in, bf16[1280,256]{1,0:T(8,128)(2,1)} %copy-done.2, ...), custom_call_target="tpu_custom_call" | custom-call | tf_op jit(solution)/shard_map/conv_backward/pallas_call | solution.py:1205
  291.8 1.8 bitcast_convert_fusion
  293.6 6.0 %convert_bitcast_fusion = f32[256,27,256]{2,0,1:T(8,128)} fusion(bf16[29,256,256]{2,1,0:T(8,128)(2,1)} %get-tuple-element.36), kind=kLoop, calls=%fused_computation | loop fusion | flops 1769472 | bytes 10616832 | tf_op jit(solution)/shard_map/transpose | solution.py:1340
  299.6 1.0 copy.48
  300.6 0.7 copy.49
  301.3 0.6 copy.50
  301.9 0.6 copy.51
  (36 shorter events, 0.2 us)
Async XLA Ops:
  2.3 2.2 copy-start.12
  2.3 2.2 copy-start.13
  2.3 2.9 copy-start.11
  2.4 3.6 %copy-start.14 = (bf16[160,256]{1,0:T(8,128)(2,1)S(1)}, bf16[160,256]{1,0:T(8,128)(2,1)}, u32[]{:S(2)}) copy-start(bf16[160,256]{1,0:T(8,128)(2,1)} %param.20) | copy-start | bytes 245764
  2.4 4.3 %copy-start.15 = (s32[5]{0:T(128)S(1)}, s32[5]{0:T(128)}, u32[]{:S(2)}) copy-start(s32[5]{0:T(128)} %param.15) | copy-start | bytes 64
  2.4 4.5 %copy-start.16 = (s32[5]{0:T(128)S(1)}, s32[5]{0:T(128)}, u32[]{:S(2)}) copy-start(s32[5]{0:T(128)} %param.16) | copy-start | bytes 64
  10.2 102.9 %copy-start.4 = (bf16[128,112]{1,0:T(8,128)(2,1)S(1)}, bf16[128,112]{1,0:T(8,128)(2,1)}, u32[]{:S(2)}) copy-start(bf16[128,112]{1,0:T(8,128)(2,1)} %constant.66.clone.sel_t) | copy-start | bytes 86020
  10.2 102.9 %copy-start.6 = (f32[6,256]{1,0:T(8,128)S(1)}, f32[6,256]{1,0:T(8,128)}, u32[]{:S(2)}) copy-start(f32[6,256]{1,0:T(8,128)} %gains.1) | copy-start | bytes 18436
  10.2 102.9 %copy-start.7 = (f32[6,256]{1,0:T(8,128)S(1)}, f32[6,256]{1,0:T(8,128)}, u32[]{:S(2)}) copy-start(f32[6,256]{1,0:T(8,128)} %biases.1) | copy-start | bytes 18436
  110.4 2.7 copy-start
  113.1 0.9 copy-start.3
  114.1 0.7 copy-start.5
  151.8 0.8 copy-start.1
  152.6 0.8 copy-start.2
  153.4 0.7 copy-start.8
  293.6 6.0 %copy-start.9 = (bf16[13,24,2048]{2,1,0:T(8,128)(2,1)S(1)}, bf16[13,24,2048]{2,1,0:T(8,128)(2,1)}, u32[]{:S(2)}) copy-start(bf16[13,24,2048]{2,1,0:T(8,128)(2,1)} %get-tuple-element.35) | copy-start | bytes 3833860
  293.6 7.0 %copy-start.10 = (f32[160,256]{1,0:T(8,128)S(1)}, f32[160,256]{1,0:T(8,128)}, u32[]{:S(2)}) copy-start(f32[160,256]{1,0:T(8,128)} %get-tuple-element.89) | copy-start | bytes 491524
